TPU v7x, 128 devices: a whole 4x4x4 slice. The times are simulated.
128 devices in a mesh: dp: 32 (over z, x, core), tensor: 4 (over y).
Axes of the slice: x: 4, y: 4, z: 4, core: 2. Of those that a mesh axis runs over, the one named last changes fastest.
Arguments:
- tokens: bfloat16 [16384, 1152], P(('dp', 'tensor')), may hold values from -6 to 6
- document_ids: int32 [16384], P('dp'), may hold values from -1 to 127, as said below
- cotangent: bfloat16 [16384, 1152], P(('dp', 'tensor')), may hold values from -6 to 6
- query_weight: float32 [1152, 1024], P('dp', 'tensor'), may hold values from -0.1875 to 0.1875
- keyvalue_weight: float32 [1152, 512], P('dp'), may hold values from -0.1875 to 0.1875
- output_weight: float32 [1024, 1152], P('tensor', 'dp'), may hold values from -0.1875 to 0.1875
- gate_weight: float32 [1152, 6912], P('dp', 'tensor'), may hold values from -0.1875 to 0.1875
- up_weight: float32 [1152, 6912], P('dp', 'tensor'), may hold values from -0.1875 to 0.1875
- down_weight: float32 [6912, 1152], P('tensor', 'dp'), may hold values from -0.078125 to 0.078125
- norm_gains: float32 [5120], P('dp'), may hold values from 0.5 to 1.5
- query_first: float32 [1152, 1024], P('dp', 'tensor'), may hold values from -80 to 80
- query_second: float32 [1152, 1024], P('dp', 'tensor'), may hold values from 425.984 to 6881.28
- keyvalue_first: float32 [1152, 512], P('dp'), may hold values from -80 to 80
- keyvalue_second: float32 [1152, 512], P('dp'), may hold values from 425.984 to 6881.28
- output_first: float32 [1024, 1152], P('tensor', 'dp'), may hold values from -80 to 80
- output_second: float32 [1024, 1152], P('tensor', 'dp'), may hold values from 425.984 to 6881.28
- gate_first: float32 [1152, 6912], P('dp', 'tensor'), may hold values from -40 to 40
- gate_second: float32 [1152, 6912], P('dp', 'tensor'), may hold values from 108.1344 to 1720.32
- up_first: float32 [1152, 6912], P('dp', 'tensor'), may hold values from -40 to 40
- up_second: float32 [1152, 6912], P('dp', 'tensor'), may hold values from 108.1344 to 1720.32
- down_first: float32 [6912, 1152], P('tensor', 'dp'), may hold values from -80 to 80
- down_second: float32 [6912, 1152], P('tensor', 'dp'), may hold values from 425.984 to 6881.28
- gain_first: float32 [5120], P('dp'), may hold values from -80 to 80
- gain_second: float32 [5120], P('dp'), may hold values from 425.984 to 6881.28
Outputs:
- block_output: bfloat16 [16384, 1152], P(('dp', 'tensor'))
- token_grad: bfloat16 [16384, 1152], P(('dp', 'tensor'))
- query_first_next: float32 [1152, 1024], P('dp', 'tensor')
- query_second_next: float32 [1152, 1024], P('dp', 'tensor')
- query_weight_next: float32 [1152, 1024], P('dp', 'tensor')
- keyvalue_first_next: float32 [1152, 512], P('dp')
- keyvalue_second_next: float32 [1152, 512], P('dp')
- keyvalue_weight_next: float32 [1152, 512], P('dp')
- output_first_next: float32 [1024, 1152], P('tensor', 'dp')
- output_second_next: float32 [1024, 1152], P('tensor', 'dp')
- output_weight_next: float32 [1024, 1152], P('tensor', 'dp')
- gate_first_next: float32 [1152, 6912], P('dp', 'tensor')
- gate_second_next: float32 [1152, 6912], P('dp', 'tensor')
- gate_weight_next: float32 [1152, 6912], P('dp', 'tensor')
- up_first_next: float32 [1152, 6912], P('dp', 'tensor')
- up_second_next: float32 [1152, 6912], P('dp', 'tensor')
- up_weight_next: float32 [1152, 6912], P('dp', 'tensor')
- down_first_next: float32 [6912, 1152], P('tensor', 'dp')
- down_second_next: float32 [6912, 1152], P('tensor', 'dp')
- down_weight_next: float32 [6912, 1152], P('tensor', 'dp')
- gain_first_next: float32 [5120], P('dp')
- gain_second_next: float32 [5120], P('dp')
- norm_gains_next: float32 [5120], P('dp')
Inputs may be any that keep to these rules, and one draw needn't show every extreme that they name: `document_ids`: each pack of 512 tokens starts with document 0, which is longer than 384 tokens; ids never fall within a pack and count up by one from document to document; a pack's last positions, at most 64 of them, may be padding (-1); in every draw some pack is a single document of 512 tokens, and some pack ends in documents of one token each.
All inputs are finite; a program needn't handle non-finite values.
Results may differ from a plain program's by a relative error of at most 0.035.
Values may be sent and summed in bfloat16 or wider, within the bound.
A program may use at most 128 MiB of HBM per device.

v0:
```python
import jax
import jax.numpy as jnp
from jax import lax
from jax.sharding import PartitionSpec as P

D = 1152
H = 4
HD = 256
FF = 6912
STEP = 10


norm_epsilon = 1e-06
rope_base = 1000000.0
beta_first = 0.9
beta_second = 0.95
adam_epsilon = 1e-08
weight_decay = 0.1
matrix_rate = 2.0
gain_rate = 1.0


def root_norm(values, gain):
    return (
        values * lax.rsqrt(jnp.mean(values * values, axis=-1, keepdims=True) + norm_epsilon) * gain
    )


def document_positions(document_ids):
    length = document_ids.shape[0]
    index = jnp.arange(length, dtype=jnp.int32)
    changed = jnp.concatenate([jnp.ones((1,), dtype=bool), document_ids[1:] != document_ids[:-1]])
    starts = lax.cummax(jnp.where(changed, index, jnp.zeros_like(index)), axis=0)
    return index - starts


def rope_tables(positions, width):
    half_width = width // 2
    exponent = jnp.arange(half_width, dtype=jnp.float32) * (2.0 / width)
    frequency = rope_base ** (-exponent)
    angle_table = positions.astype(jnp.float32)[:, None] * frequency[None, :]
    return (jnp.cos(angle_table), jnp.sin(angle_table))


def rotate(values, cosine_part, sine_part):
    half_width = values.shape[-1] // 2
    former = values[..., :half_width]
    latter = values[..., half_width:]
    return jnp.concatenate(
        [former * cosine_part - latter * sine_part, latter * cosine_part + former * sine_part],
        axis=-1,
    )


def allowed_block(document_ids, first_row, span_rows):
    length = document_ids.shape[0]
    query_index = first_row + jnp.arange(span_rows, dtype=jnp.int32)
    key_index = jnp.arange(length, dtype=jnp.int32)
    same = (
        (document_ids[:, None] == document_ids[None, :])
        & (document_ids[:, None] >= 0)
        & (key_index[None, :] <= query_index[:, None])
    )
    return same | (key_index[None, :] == query_index[:, None])


def gated_gelu(gate_values, up_values):
    return jax.nn.gelu(gate_values, approximate=True) * up_values


def adam_update(weight, gradient, first, second, rate, decay_rate):
    first_new = beta_first * first + (1.0 - beta_first) * gradient
    second_new = beta_second * second + (1.0 - beta_second) * gradient * gradient
    first_hat = first_new / (1.0 - beta_first**STEP)
    second_hat = second_new / (1.0 - beta_second**STEP)
    weight_new = weight - rate * (
        first_hat / (jnp.sqrt(second_hat) + adam_epsilon) + decay_rate * weight
    )
    return (first_new, second_new, weight_new)


def per_device(
    tokens,
    document_ids,
    cotangent,
    query_weight,
    keyvalue_weight,
    output_weight,
    gate_weight,
    up_weight,
    down_weight,
    norm_gains,
    query_first,
    query_second,
    keyvalue_first,
    keyvalue_second,
    output_first,
    output_second,
    gate_first,
    gate_second,
    up_first,
    up_second,
    down_first,
    down_second,
    gain_first,
    gain_second,
):
    row_count = tokens.shape[0]
    pack_rows = document_ids.shape[0]
    block_rows = min(512, pack_rows)
    block_count = pack_rows // block_rows
    local_heads = query_weight.shape[1] // HD
    own_start = lax.axis_index("tensor") * row_count
    scale_factor = HD ** (-0.5)
    block_starts = jnp.arange(block_count, dtype=jnp.int32) * block_rows
    query_full, keyvalue_full, output_full, gate_full, up_full, down_full, gain_full = (
        lax.all_gather(query_weight.astype(jnp.bfloat16), "dp", axis=0, tiled=True),
        lax.all_gather(keyvalue_weight.astype(jnp.bfloat16), "dp", axis=0, tiled=True),
        lax.all_gather(output_weight.astype(jnp.bfloat16), "dp", axis=1, tiled=True),
        lax.all_gather(gate_weight.astype(jnp.bfloat16), "dp", axis=0, tiled=True),
        lax.all_gather(up_weight.astype(jnp.bfloat16), "dp", axis=0, tiled=True),
        lax.all_gather(down_weight.astype(jnp.bfloat16), "dp", axis=1, tiled=True),
        lax.all_gather(norm_gains.astype(jnp.bfloat16), "dp", axis=0, tiled=True),
    )
    gain_values = gain_full.astype(jnp.float32)
    pre_attn = gain_values[0:D]
    post_attn = gain_values[D : 2 * D]
    pre_ffn = gain_values[2 * D : 3 * D]
    post_ffn = gain_values[3 * D : 4 * D]
    query_gain = gain_values[4 * D : 4 * D + HD]
    key_gain = gain_values[4 * D + HD : 4 * D + 2 * HD]
    cosine_part, sine_part = rope_tables(document_positions(document_ids), HD)
    inputs = tokens.astype(jnp.float32)
    normed_local, pre_attn_pull = jax.vjp(root_norm, inputs, pre_attn)
    normed_full = lax.all_gather(normed_local.astype(jnp.bfloat16), "tensor", axis=0, tiled=True)
    query_raw = jnp.dot(normed_full, query_full, preferred_element_type=jnp.float32)
    keyvalue_raw = jnp.dot(normed_full, keyvalue_full, preferred_element_type=jnp.float32)
    query_heads = jnp.transpose(query_raw.reshape(pack_rows, local_heads, HD), (1, 0, 2))

    def query_shape(query_values, query_scale):
        return rotate(root_norm(query_values, query_scale), cosine_part, sine_part)

    query_rot, query_pull = jax.vjp(query_shape, query_heads, query_gain)
    key_raw = keyvalue_raw[:, :HD]

    def key_shape(key_values):
        return rotate(root_norm(key_values, key_gain), cosine_part, sine_part)

    key_rot, key_pull = jax.vjp(key_shape, key_raw)
    query_low = query_rot.astype(jnp.bfloat16)
    key_low = key_rot.astype(jnp.bfloat16)
    value_low = keyvalue_raw[:, HD:].astype(jnp.bfloat16)

    def attend_block(first_row):
        scores = (
            jnp.einsum("hqd,kd->hqk", query_low, key_low, preferred_element_type=jnp.float32)
            * scale_factor
        )
        scores = jnp.where(allowed_block(document_ids, first_row, block_rows)[None], scores, -1e30)
        row_peak = jnp.max(scores, axis=-1, keepdims=True)
        exponents = jnp.exp(scores - row_peak)
        row_total = jnp.sum(exponents, axis=-1, keepdims=True)
        probabilities = (exponents / row_total).astype(jnp.bfloat16)
        head_block = jnp.einsum(
            "hqk,kd->hqd", probabilities, value_low, preferred_element_type=jnp.float32
        ).astype(jnp.bfloat16)
        return (head_block, row_peak[..., 0] + jnp.log(row_total[..., 0]))

    head_blocks, total_blocks = lax.map(attend_block, block_starts)
    heads_out = jnp.transpose(head_blocks, (1, 0, 2, 3)).reshape(local_heads, pack_rows, HD)
    log_totals = jnp.transpose(total_blocks, (1, 0, 2)).reshape(local_heads, pack_rows)
    merged = jnp.transpose(heads_out, (1, 0, 2)).reshape(pack_rows, local_heads * HD)
    attention_local = lax.psum_scatter(
        jnp.dot(merged, output_full, preferred_element_type=jnp.float32).astype(jnp.bfloat16),
        "tensor",
        scatter_dimension=0,
        tiled=True,
    ).astype(jnp.float32)
    attention_normed, post_attn_pull = jax.vjp(root_norm, attention_local, post_attn)
    middle = inputs + attention_normed
    ffn_normed_local, pre_ffn_pull = jax.vjp(root_norm, middle, pre_ffn)
    ffn_full = lax.all_gather(ffn_normed_local.astype(jnp.bfloat16), "tensor", axis=0, tiled=True)
    gate_values = jnp.dot(ffn_full, gate_full, preferred_element_type=jnp.float32)
    up_values = jnp.dot(ffn_full, up_full, preferred_element_type=jnp.float32)
    hidden_values, gelu_pull = jax.vjp(gated_gelu, gate_values, up_values)
    hidden_low = hidden_values.astype(jnp.bfloat16)
    ffn_local = lax.psum_scatter(
        jnp.dot(hidden_low, down_full, preferred_element_type=jnp.float32).astype(jnp.bfloat16),
        "tensor",
        scatter_dimension=0,
        tiled=True,
    ).astype(jnp.float32)
    ffn_normed_out, post_ffn_pull = jax.vjp(root_norm, ffn_local, post_ffn)
    block_output = (middle + ffn_normed_out).astype(jnp.bfloat16)
    query_full, keyvalue_full, output_full, gate_full, up_full, down_full = (
        lax.all_gather(query_weight.astype(jnp.bfloat16), "dp", axis=0, tiled=True),
        lax.all_gather(keyvalue_weight.astype(jnp.bfloat16), "dp", axis=0, tiled=True),
        lax.all_gather(output_weight.astype(jnp.bfloat16), "dp", axis=1, tiled=True),
        lax.all_gather(gate_weight.astype(jnp.bfloat16), "dp", axis=0, tiled=True),
        lax.all_gather(up_weight.astype(jnp.bfloat16), "dp", axis=0, tiled=True),
        lax.all_gather(down_weight.astype(jnp.bfloat16), "dp", axis=1, tiled=True),
    )
    own_docs = lax.dynamic_slice_in_dim(document_ids, own_start, row_count, 0)
    upstream = cotangent.astype(jnp.float32) * (own_docs >= 0).astype(jnp.float32)[:, None]
    ffn_out_grad, post_ffn_grad = post_ffn_pull(upstream)
    ffn_out_full = lax.all_gather(ffn_out_grad.astype(jnp.bfloat16), "tensor", axis=0, tiled=True)
    hidden_grad = jnp.einsum(
        "rd,fd->rf", ffn_out_full, down_full, preferred_element_type=jnp.float32
    )
    down_weight_grad = jnp.einsum(
        "rf,rd->fd", hidden_low, ffn_out_full, preferred_element_type=jnp.float32
    )
    gate_value_grad, up_value_grad = gelu_pull(hidden_grad)
    gate_low = gate_value_grad.astype(jnp.bfloat16)
    up_low = up_value_grad.astype(jnp.bfloat16)
    gate_weight_grad = jnp.einsum(
        "rd,rf->df", ffn_full, gate_low, preferred_element_type=jnp.float32
    )
    up_weight_grad = jnp.einsum("rd,rf->df", ffn_full, up_low, preferred_element_type=jnp.float32)
    ffn_normed_grad = lax.psum_scatter(
        (
            jnp.einsum("rf,df->rd", gate_low, gate_full, preferred_element_type=jnp.float32)
            + jnp.einsum("rf,df->rd", up_low, up_full, preferred_element_type=jnp.float32)
        ).astype(jnp.bfloat16),
        "tensor",
        scatter_dimension=0,
        tiled=True,
    ).astype(jnp.float32)
    middle_part, pre_ffn_grad = pre_ffn_pull(ffn_normed_grad)
    middle_grad = upstream + middle_part
    attention_grad, post_attn_grad = post_attn_pull(middle_grad)
    attention_full = lax.all_gather(
        attention_grad.astype(jnp.bfloat16), "tensor", axis=0, tiled=True
    )
    output_weight_grad = jnp.einsum(
        "rc,rd->cd", merged, attention_full, preferred_element_type=jnp.float32
    )
    merged_grad = jnp.einsum(
        "rd,cd->rc", attention_full, output_full, preferred_element_type=jnp.float32
    ).astype(jnp.bfloat16)
    heads_grad = jnp.transpose(merged_grad.reshape(pack_rows, local_heads, HD), (1, 0, 2))

    def attention_back(running, first_row):
        key_partial, value_partial = running
        scores = (
            jnp.einsum("hqd,kd->hqk", query_low, key_low, preferred_element_type=jnp.float32)
            * scale_factor
        )
        scores = jnp.where(allowed_block(document_ids, first_row, block_rows)[None], scores, -1e30)
        probabilities = jnp.exp(scores - log_totals[..., None])
        probability_grad = jnp.einsum(
            "hqd,kd->hqk", heads_grad, value_low, preferred_element_type=jnp.float32
        )
        score_low = (
            probabilities
            * (probability_grad - jnp.sum(probabilities * probability_grad, axis=-1, keepdims=True))
        ).astype(jnp.bfloat16)
        query_block_grad = (
            jnp.einsum("hqk,kd->hqd", score_low, key_low, preferred_element_type=jnp.float32)
            * scale_factor
        )
        key_partial = (
            key_partial
            + jnp.einsum("hqk,hqd->kd", score_low, query_low, preferred_element_type=jnp.float32)
            * scale_factor
        )
        value_partial = value_partial + jnp.einsum(
            "hqk,hqd->kd",
            probabilities.astype(jnp.bfloat16),
            heads_grad,
            preferred_element_type=jnp.float32,
        )
        return ((key_partial, value_partial), query_block_grad)

    zero_rows = jnp.zeros((pack_rows, HD), jnp.float32)
    (key_partial, value_partial), query_grad_blocks = lax.scan(
        attention_back, (zero_rows, zero_rows), block_starts
    )
    query_rot_grad = jnp.transpose(query_grad_blocks, (1, 0, 2, 3)).reshape(
        local_heads, pack_rows, HD
    )
    key_total, value_total = (
        lax.psum(key_partial.astype(jnp.bfloat16), "tensor").astype(jnp.float32),
        lax.psum(value_partial.astype(jnp.bfloat16), "tensor").astype(jnp.float32),
    )
    query_raw_grad, query_gain_grad = query_pull(query_rot_grad)
    (key_raw_grad,) = key_pull(key_total)
    key_raw_own = lax.dynamic_slice_in_dim(key_raw, own_start, row_count, 0)
    cosine_own = lax.dynamic_slice_in_dim(cosine_part, own_start, row_count, 0)
    sine_own = lax.dynamic_slice_in_dim(sine_part, own_start, row_count, 0)

    def key_own_shape(key_scale):
        return rotate(root_norm(key_raw_own, key_scale), cosine_own, sine_own)

    unused, key_gain_pull = jax.vjp(key_own_shape, key_gain)
    (key_gain_grad,) = key_gain_pull(lax.dynamic_slice_in_dim(key_total, own_start, row_count, 0))
    query_grad_low = (
        jnp.transpose(query_raw_grad, (1, 0, 2))
        .reshape(pack_rows, local_heads * HD)
        .astype(jnp.bfloat16)
    )
    keyvalue_grad_low = jnp.concatenate([key_raw_grad, value_total], axis=1).astype(jnp.bfloat16)
    query_weight_grad = jnp.einsum(
        "rd,rc->dc", normed_full, query_grad_low, preferred_element_type=jnp.float32
    )
    keyvalue_weight_grad = jnp.einsum(
        "rd,rc->dc", normed_full, keyvalue_grad_low, preferred_element_type=jnp.float32
    )
    normed_grad = lax.psum_scatter(
        jnp.einsum(
            "rc,dc->rd", query_grad_low, query_full, preferred_element_type=jnp.float32
        ).astype(jnp.bfloat16),
        "tensor",
        scatter_dimension=0,
        tiled=True,
    ).astype(jnp.float32)
    keyvalue_own = lax.dynamic_slice_in_dim(keyvalue_grad_low, own_start, row_count, 0)
    normed_grad = normed_grad + jnp.einsum(
        "rc,dc->rd", keyvalue_own, keyvalue_full, preferred_element_type=jnp.float32
    )
    inputs_grad, pre_attn_grad = pre_attn_pull(normed_grad)
    token_grad = (middle_grad + inputs_grad).astype(jnp.bfloat16)
    gain_grad = jnp.concatenate(
        [pre_attn_grad, post_attn_grad, pre_ffn_grad, post_ffn_grad, query_gain_grad, key_gain_grad]
    )
    query_shard, keyvalue_shard, output_shard, gate_shard, up_shard, down_shard, gain_shard = (
        lax.psum_scatter(
            query_weight_grad.astype(jnp.bfloat16), "dp", scatter_dimension=0, tiled=True
        ).astype(jnp.float32),
        lax.psum_scatter(
            keyvalue_weight_grad.astype(jnp.bfloat16), "dp", scatter_dimension=0, tiled=True
        ).astype(jnp.float32),
        lax.psum_scatter(
            output_weight_grad.astype(jnp.bfloat16), "dp", scatter_dimension=1, tiled=True
        ).astype(jnp.float32),
        lax.psum_scatter(
            gate_weight_grad.astype(jnp.bfloat16), "dp", scatter_dimension=0, tiled=True
        ).astype(jnp.float32),
        lax.psum_scatter(
            up_weight_grad.astype(jnp.bfloat16), "dp", scatter_dimension=0, tiled=True
        ).astype(jnp.float32),
        lax.psum_scatter(
            down_weight_grad.astype(jnp.bfloat16), "dp", scatter_dimension=1, tiled=True
        ).astype(jnp.float32),
        lax.psum_scatter(
            gain_grad.astype(jnp.bfloat16), "dp", scatter_dimension=0, tiled=True
        ).astype(jnp.float32),
    )
    gain_total = lax.psum(gain_shard, "tensor")
    query_next = adam_update(
        query_weight,
        query_shard,
        query_first,
        query_second,
        matrix_rate * D ** (-0.5),
        weight_decay,
    )
    keyvalue_next = adam_update(
        keyvalue_weight,
        keyvalue_shard,
        keyvalue_first,
        keyvalue_second,
        matrix_rate * D ** (-0.5),
        weight_decay,
    )
    output_next = adam_update(
        output_weight,
        output_shard,
        output_first,
        output_second,
        matrix_rate * (H * HD) ** (-0.5),
        weight_decay,
    )
    gate_next = adam_update(
        gate_weight, gate_shard, gate_first, gate_second, matrix_rate * D ** (-0.5), weight_decay
    )
    up_next = adam_update(
        up_weight, up_shard, up_first, up_second, matrix_rate * D ** (-0.5), weight_decay
    )
    down_next = adam_update(
        down_weight, down_shard, down_first, down_second, matrix_rate * FF ** (-0.5), weight_decay
    )
    gain_next = adam_update(norm_gains, gain_total, gain_first, gain_second, gain_rate, 0.0)
    return (
        block_output,
        token_grad,
        query_next[0],
        query_next[1],
        query_next[2],
        keyvalue_next[0],
        keyvalue_next[1],
        keyvalue_next[2],
        output_next[0],
        output_next[1],
        output_next[2],
        gate_next[0],
        gate_next[1],
        gate_next[2],
        up_next[0],
        up_next[1],
        up_next[2],
        down_next[0],
        down_next[1],
        down_next[2],
        gain_next[0],
        gain_next[1],
        gain_next[2],
    )


def solution(mesh):
    placed = (
        P(("dp", "tensor"), None),
        P("dp"),
        P(("dp", "tensor"), None),
        P("dp", "tensor"),
        P("dp", None),
        P("tensor", "dp"),
        P("dp", "tensor"),
        P("dp", "tensor"),
        P("tensor", "dp"),
        P("dp"),
        P("dp", "tensor"),
        P("dp", "tensor"),
        P("dp", None),
        P("dp", None),
        P("tensor", "dp"),
        P("tensor", "dp"),
        P("dp", "tensor"),
        P("dp", "tensor"),
        P("dp", "tensor"),
        P("dp", "tensor"),
        P("tensor", "dp"),
        P("tensor", "dp"),
        P("dp"),
        P("dp"),
    )
    return jax.shard_map(
        per_device,
        mesh=mesh,
        in_specs=placed,
        out_specs=(
            P(("dp", "tensor"), None),
            P(("dp", "tensor"), None),
            P("dp", "tensor"),
            P("dp", "tensor"),
            P("dp", "tensor"),
            P("dp", None),
            P("dp", None),
            P("dp", None),
            P("tensor", "dp"),
            P("tensor", "dp"),
            P("tensor", "dp"),
            P("dp", "tensor"),
            P("dp", "tensor"),
            P("dp", "tensor"),
            P("dp", "tensor"),
            P("dp", "tensor"),
            P("dp", "tensor"),
            P("tensor", "dp"),
            P("tensor", "dp"),
            P("tensor", "dp"),
            P("dp"),
            P("dp"),
            P("dp"),
        ),
        check_vma=False,
    )
```

profile of v0, /device:TPU:0, one launch (start us, length us, event | category | flops | bytes accessed | tf_op | source)
XLA Modules:
  0.0 962.0 jit_solution(11348335213840109702)
XLA Ops:
  10.2 129.5 %all-reduce.6 = bf16[5120]{0:T(1024)(128)(2,1)S(1)} all-reduce(bf16[5120]{0:T(1024)(128)(2,1)S(1)} %dynamic-update-slice), channel_id=1, replica_groups=mesh['dp'=32,'tensor'=4] {'dp'}, use_global_device_ids=true, to_apply=%add.6 | all-reduce | flops 5120 | bytes 20480
  146.0 21.8 %all-gather = bf16[32,36,256]{2,1,0:T(8,128)(2,1)S(1)} all-gather(bf16[1,36,256]{2,1,0:T(8,128)(2,1)S(1)} %convert_bitcast_fusion.5), channel_id=1, replica_groups=mesh['dp'=32,'tensor'=4] {'dp'}, dimensions={0}, use_global_device_ids=true | all-gather | bytes 608256 | tf_op jit(solution)/shard_map/all_gather | solution.py:117
  168.5 25.0 %all-gather.2 = bf16[32,36,256]{2,1,0:T(8,128)(2,1)S(1)} all-gather(bf16[1,36,256]{2,1,0:T(8,128)(2,1)S(1)} %convert_bitcast_fusion.4), channel_id=1, replica_groups=mesh['dp'=32,'tensor'=4] {'dp'}, dimensions={0}, use_global_device_ids=true | all-gather | bytes 608256 | tf_op jit(solution)/shard_map/all_gather | solution.py:119
  197.9 12.4 %all-gather.23.cloned.1.call-done = bf16[32,36,512]{2,1,0:T(8,128)(2,1)} async-done(((bf16[1,36,512]{2,1,0:T(8,128)(2,1)}), bf16[32,36,512]{2,1,0:T(8,128)(2,1)}) %all-gather.23.cloned.1.call-update) | async-done | bytes 1179664 | tf_op jit(solution)/shard_map/all_gather | solution.py:118
  225.0 20.2 %reduce-scatter.17.cloned.1.call-done = bf16[128,1152]{1,0:T(8,128)(2,1)} async-done(((bf16[512,1152]{1,0:T(8,128)(2,1)}), bf16[128,1152]{1,0:T(8,128)(2,1)}) %reduce-scatter.17.cloned.1.call-update) | async-done | bytes 294928 | tf_op jit(solution)/shard_map/reduce_scatter | solution.py:173
  250.5 44.2 %all-gather.25.cloned.1.call-done = bf16[32,36,1728]{2,1,0:T(8,128)(2,1)} async-done(((bf16[1,36,1728]{2,1,0:T(8,128)(2,1)}), bf16[32,36,1728]{2,1,0:T(8,128)(2,1)}) %all-gather.25.cloned.1.call-update) | async-done | bytes 3981328 | tf_op jit(solution)/shard_map/all_gather | solution.py:120
  294.7 7.3 reshape.418
  302.0 41.7 %all-gather.27.cloned.1.call-done = bf16[32,36,1728]{2,1,0:T(8,128)(2,1)} async-done(((bf16[1,36,1728]{2,1,0:T(8,128)(2,1)}), bf16[32,36,1728]{2,1,0:T(8,128)(2,1)}) %all-gather.27.cloned.1.call-update) | async-done | bytes 3981328 | tf_op jit(solution)/shard_map/all_gather | solution.py:121
  343.7 7.3 reshape.420
  351.0 41.7 %all-gather.29.cloned.1.call-done = bf16[32,36,1728]{2,1,0:T(8,128)(2,1)} async-done(((bf16[1,36,1728]{2,1,0:T(8,128)(2,1)}), bf16[32,36,1728]{2,1,0:T(8,128)(2,1)}) %all-gather.29.cloned.1.call-update) | async-done | bytes 3981328 | tf_op jit(solution)/shard_map/all_gather | solution.py:122
  392.7 7.3 reshape.422
  400.0 18.7 %all-gather.17.cloned.1.call-done = bf16[512,1152]{1,0:T(8,128)(2,1)} async-done(((bf16[128,1152]{1,0:T(8,128)(2,1)}), bf16[512,1152]{1,0:T(8,128)(2,1)}) %all-gather.17.cloned.1.call-update) | async-done | bytes 1179664 | tf_op jit(solution)/shard_map/all_gather | solution.py:182
  434.9 24.0 %reduce-scatter.19.cloned.1.call-done = bf16[128,1152]{1,0:T(8,128)(2,1)} async-done(((bf16[512,1152]{1,0:T(8,128)(2,1)}), bf16[128,1152]{1,0:T(8,128)(2,1)}) %reduce-scatter.19.cloned.1.call-update) | async-done | bytes 294928 | tf_op jit(solution)/shard_map/reduce_scatter | solution.py:187
  464.1 24.1 %all-gather.19.cloned.1.call-done = bf16[512,1152]{1,0:T(8,128)(2,1)} async-done(((bf16[128,1152]{1,0:T(8,128)(2,1)}), bf16[512,1152]{1,0:T(8,128)(2,1)}) %all-gather.19.cloned.1.call-update) | async-done | bytes 1179664 | tf_op jit(solution)/shard_map/all_gather | solution.py:206
  488.1 9.7 %multiply_convert_fusion = (bf16[512,1728]{0,1:T(8,128)(2,1)S(1)}, bf16[512,1728]{0,1:T(8,128)(2,1)S(1)}) fusion(f32[512,1728]{0,1:T(8,128)} %copy-done.85, f32[512,1728]{0,1:T(8,128)} %get-tuple-element.153, bf16[512,1152]{1,0:T(8,128)(2,1)} %all-gather.19.cloned.1.call-done, bf16[1152,1728]{1,0:T(8,128)(2,1)} %reshape.422), kind=kOutput, calls=%fused_computation.12 | convolution fusion | flops 2059665408 | bytes 15777792 | tf_op jit(solution)/shard_map/rd,fd->rf/dot_general | solution.py:207
  507.9 21.9 %reduce-scatter.21.cloned.1.call-done = bf16[128,1152]{1,0:T(8,128)(2,1)} async-done(((bf16[512,1152]{1,0:T(8,128)(2,1)}), bf16[128,1152]{1,0:T(8,128)(2,1)}) %reduce-scatter.21.cloned.1.call-update) | async-done | bytes 294928 | tf_op jit(solution)/shard_map/reduce_scatter | solution.py:220
  539.3 6.3 convolution_convert_fusion
  554.4 7.1 all-gather.21.cloned.1.call-done
  575.9 36.8 %all-reduce.24.cloned.1.call-done = (bf16[512,256]{0,1:T(8,128)(2,1)}, bf16[512,256]{0,1:T(8,128)(2,1)}) async-done(((bf16[512,256]{0,1:T(8,128)(2,1)}, bf16[512,256]{0,1:T(8,128)(2,1)}), (bf16[512,256]{0,1:T(8,128)(2,1)}, bf16[512,256]{0,1:T(8,128)(2,1)})) %all-reduce.24.cloned.1.call-update) | async-done | bytes 524304 | tf_op jit(solution)/shard_map/psum | solution.py:283
  617.9 97.2 %fusion.115 = (bf16[40,256]{1,0:T(8,128)(2,1)S(1)}, bf16[40,512]{1,0:T(8,128)(2,1)S(1)}, bf16[256,40]{0,1:T(8,128)(2,1)S(1)}, bf16[40,1728]{1,0:T(8,128)(2,1)S(1...) fusion(bf16[1152,256]{1,0:T(8,128)(2,1)} %convolution_convert_fusion.8, ...), kind=kCustom, calls=%all-reduce-scatter.6 | all-reduce-scatter fusion | flops 7946241 | bytes 14800384
  796.6 6.8 concatenate.41
  803.4 6.8 concatenate.40
  820.2 123.8 %all-reduce.13 = bf16[5120]{0:T(1024)(128)(2,1)S(1)} all-reduce(bf16[5120]{0:T(1024)(128)(2,1)S(1)} %dynamic-update-slice.6), channel_id=12, replica_groups=mesh['dp'=32,'tensor'=4] {'dp'}, use_global_device_ids=true, to_apply=%region_36.37.clone | all-reduce | flops 5120 | bytes 20480
  944.1 9.4 psum.23
  (373 shorter events, 193.4 us)
Async XLA Ops:
  7.2 187.5 %all-gather.15.cloned.1.call-start = ((), (), s32[]{:S(2)}) async-start(), calls=%async_computation.4 | async-start | bytes 1474560 | tf_op jit(solution)/shard_map/all_gather | solution.py:135
  142.7 67.6 %all-gather.23.cloned.1.call-start = ((), (), s32[]{:S(2)}) async-start(), calls=%async_computation.12 | async-start | bytes 1351680 | tf_op jit(solution)/shard_map/all_gather | solution.py:118
  144.3 100.8 %reduce-scatter.17.cloned.1.call-start = ((), (), s32[]{:S(2)}) async-start(), calls=%async_computation.5 | async-start | bytes 1474560 | tf_op jit(solution)/shard_map/reduce_scatter | solution.py:173
  221.7 73.0 %all-gather.25.cloned.1.call-start = ((), (), s32[]{:S(2)}) async-start(), calls=%async_computation.13 | async-start | bytes 4730880 | tf_op jit(solution)/shard_map/all_gather | solution.py:120
  223.4 120.3 %all-gather.27.cloned.1.call-start = ((), (), s32[]{:S(2)}) async-start(), calls=%async_computation.14 | async-start | bytes 4730880 | tf_op jit(solution)/shard_map/all_gather | solution.py:121
  224.2 168.6 %all-gather.29.cloned.1.call-start = ((), (), s32[]{:S(2)}) async-start(), calls=%async_computation.15 | async-start | bytes 4730880 | tf_op jit(solution)/shard_map/all_gather | solution.py:122
  224.9 193.8 %all-gather.17.cloned.1.call-start = ((), (), s32[]{:S(2)}) async-start(), calls=%async_computation.6 | async-start | bytes 1474560 | tf_op jit(solution)/shard_map/all_gather | solution.py:182
  250.0 208.8 %reduce-scatter.19.cloned.1.call-start = ((), (), s32[]{:S(2)}) async-start(), calls=%async_computation.7 | async-start | bytes 1474560 | tf_op jit(solution)/shard_map/reduce_scatter | solution.py:187
  434.1 54.1 %all-gather.19.cloned.1.call-start = ((), (), s32[]{:S(2)}) async-start(), calls=%async_computation.8 | async-start | bytes 1474560 | tf_op jit(solution)/shard_map/all_gather | solution.py:206
  463.8 66.0 %reduce-scatter.21.cloned.1.call-start = ((), (), s32[]{:S(2)}) async-start(), calls=%async_computation.9 | async-start | bytes 1474560 | tf_op jit(solution)/shard_map/reduce_scatter | solution.py:220
  505.1 56.4 %all-gather.21.cloned.1.call-start = ((), (), s32[]{:S(2)}) async-start(), calls=%async_computation.10 | async-start | bytes 1474560 | tf_op jit(solution)/shard_map/all_gather | solution.py:232
  537.2 75.5 %all-reduce.24.cloned.1.call-start = ((), (), s32[]{:S(2)}) async-start(), calls=%async_computation.16 | async-start | bytes 1048576 | tf_op jit(solution)/shard_map/psum | solution.py:283
  568.9 248.1 %reduce-scatter.23.cloned.1.call-start = ((), (), s32[]{:S(2)}) async-start(), calls=%async_computation.11 | async-start | bytes 1474560 | tf_op jit(solution)/shard_map/reduce_scatter | solution.py:309
  716.4 20.7 %collective-permute-start.8 = (bf16[256,40]{0,1:T(8,128)(2,1)S(1)}, bf16[256,40]{0,1:T(8,128)(2,1)S(1)}, u32[]{:S(2)}, u32[]{:S(2)}) collective-permute-start(bf16[256,40]{0,1:T(8,128)(2,1)S(1)} %get-tuple-element.94), channel_id=1, source_target_pairs={{0,4},{4,8},{8,12},{12,16},{16,20},{20,24},{24,28},{28,32},{32,36}... | collective-permute-start | bytes 61448
  718.5 22.7 %collective-permute-start.9 = (bf16[256,40]{0,1:T(8,128)(2,1)S(1)}, bf16[256,40]{0,1:T(8,128)(2,1)S(1)}, u32[]{:S(2)}, u32[]{:S(2)}) collective-permute-start(bf16[256,40]{0,1:T(8,128)(2,1)S(1)} %get-tuple-element.94), channel_id=1, source_target_pairs={{0,8},{4,12},{8,16},{12,20},{16,24},{20,28},{24,32},{28,36},{32,40... | collective-permute-start | bytes 61448
  726.1 25.6 %collective-permute-start = (bf16[40,256]{1,0:T(8,128)(2,1)S(1)}, bf16[40,256]{1,0:T(8,128)(2,1)S(1)}, u32[]{:S(2)}, u32[]{:S(2)}) collective-permute-start(bf16[40,256]{1,0:T(8,128)(2,1)S(1)} %get-tuple-element.92), channel_id=1, source_target_pairs={{0,4},{4,8},{8,12},{12,16},{16,20},{20,24},{24,28},{28,32},{32,36}... | collective-permute-start | bytes 61448
  729.5 27.2 %collective-permute-start.1 = (bf16[40,256]{1,0:T(8,128)(2,1)S(1)}, bf16[40,256]{1,0:T(8,128)(2,1)S(1)}, u32[]{:S(2)}, u32[]{:S(2)}) collective-permute-start(bf16[40,256]{1,0:T(8,128)(2,1)S(1)} %get-tuple-element.92), channel_id=1, source_target_pairs={{0,8},{4,12},{8,16},{12,20},{16,24},{20,28},{24,32},{28,36},{32,40... | collective-permute-start | bytes 61448
  732.3 29.7 %collective-permute-start.2 = (bf16[40,256]{1,0:T(8,128)(2,1)S(1)}, bf16[40,256]{1,0:T(8,128)(2,1)S(1)}, u32[]{:S(2)}, u32[]{:S(2)}) collective-permute-start(bf16[40,256]{1,0:T(8,128)(2,1)S(1)} %get-tuple-element.92), channel_id=1, source_target_pairs={{0,12},{4,16},{8,20},{12,24},{16,28},{20,32},{24,36},{28,40},{32,4... | collective-permute-start | bytes 61448
  747.0 24.0 %collective-permute-start.4 = (bf16[40,512]{1,0:T(8,128)(2,1)S(1)}, bf16[40,512]{1,0:T(8,128)(2,1)S(1)}, u32[]{:S(2)}, u32[]{:S(2)}) collective-permute-start(bf16[40,512]{1,0:T(8,128)(2,1)S(1)} %get-tuple-element.93), channel_id=1, source_target_pairs={{0,4},{4,8},{8,12},{12,16},{16,20},{20,24},{24,28},{28,32},{32,36}... | collective-permute-start | bytes 122888
  749.1 24.4 %collective-permute-start.5 = (bf16[40,512]{1,0:T(8,128)(2,1)S(1)}, bf16[40,512]{1,0:T(8,128)(2,1)S(1)}, u32[]{:S(2)}, u32[]{:S(2)}) collective-permute-start(bf16[40,512]{1,0:T(8,128)(2,1)S(1)} %get-tuple-element.93), channel_id=1, source_target_pairs={{0,8},{4,12},{8,16},{12,20},{16,24},{20,28},{24,32},{28,36},{32,40... | collective-permute-start | bytes 122888
  751.6 25.8 %collective-permute-start.6 = (bf16[40,512]{1,0:T(8,128)(2,1)S(1)}, bf16[40,512]{1,0:T(8,128)(2,1)S(1)}, u32[]{:S(2)}, u32[]{:S(2)}) collective-permute-start(bf16[40,512]{1,0:T(8,128)(2,1)S(1)} %get-tuple-element.93), channel_id=1, source_target_pairs={{0,12},{4,16},{8,20},{12,24},{16,28},{20,32},{24,36},{28,40},{32,4... | collective-permute-start | bytes 122888
  765.2 18.0 %collective-permute-start.20 = (bf16[1728,40]{0,1:T(8,128)(2,1)S(1)}, bf16[1728,40]{0,1:T(8,128)(2,1)S(1)}, u32[]{:S(2)}, u32[]{:S(2)}) collective-permute-start(bf16[1728,40]{0,1:T(8,128)(2,1)S(1)} %get-tuple-element.97), channel_id=1, source_target_pairs={{0,4},{4,8},{8,12},{12,16},{16,20},{20,24},{24,28},{28,32},{32,36}... | collective-permute-start | bytes 414728
  767.3 18.4 %collective-permute-start.21 = (bf16[1728,40]{0,1:T(8,128)(2,1)S(1)}, bf16[1728,40]{0,1:T(8,128)(2,1)S(1)}, u32[]{:S(2)}, u32[]{:S(2)}) collective-permute-start(bf16[1728,40]{0,1:T(8,128)(2,1)S(1)} %get-tuple-element.97), channel_id=1, source_target_pairs={{0,8},{4,12},{8,16},{12,20},{16,24},{20,28},{24,32},{28,36},{32,40... | collective-permute-start | bytes 414728
  785.7 17.7 %collective-permute-start.12 = (bf16[40,1728]{1,0:T(8,128)(2,1)S(1)}, bf16[40,1728]{1,0:T(8,128)(2,1)S(1)}, u32[]{:S(2)}, u32[]{:S(2)}) collective-permute-start(bf16[40,1728]{1,0:T(8,128)(2,1)S(1)} %get-tuple-element.95), channel_id=1, source_target_pairs={{0,4},{4,8},{8,12},{12,16},{16,20},{20,24},{24,28},{28,32},{32,36}... | collective-permute-start | bytes 414728
  (104 other events, 3636.9 us)
Sparse Core Ops, SparseCore 0:
  142.9 20.8 all-gather.14
  166.6 43.6 all-gather.22
  221.8 23.2 reduce-scatter.16
  247.9 46.7 all-gather.24
  297.5 46.2 all-gather.26
  346.5 46.2 all-gather.28
  395.0 23.6 all-gather.16
  434.2 24.6 reduce-scatter.18
  464.0 24.1 all-gather.18
  505.2 24.6 reduce-scatter.20
  537.3 24.1 all-gather.20
  569.0 43.6 all-reduce.23
  615.1 24.6 reduce-scatter.22
where the time goes:
time: 972 us; the launch traced here: 962 us
  blocking collectives  407 us (42%)
  waiting for transfers between devices  293 us (30%)
  starting transfers between devices  74.4 us (8%)
  matrix products  66.9 us (7%)
  other arithmetic  53.1 us (5%)
  local copies, waits for them, and re-layouts  50.3 us (5%)
  between operations  17.8 us (2%)
    unnamed x3, blocking collectives  351 us
    unnamed x24, starting transfers between devices  72.7 us
    unnamed x208, local copies, waits for them, and re-layouts  49.9 us
    all_gather x1, waiting for transfers between devices, per_device(): lax.all_gather(gate_weight.astype(jnp.bfloat16), 'dp', axis=0, tiled=True)  44.2 us
    all_gather x1, waiting for transfers between devices, per_device(): lax.all_gather(down_weight.astype(jnp.bfloat16), 'dp', axis=1, tiled=True)  41.7 us
    all_gather x1, waiting for transfers between devices, per_device(): lax.all_gather(up_weight.astype(jnp.bfloat16), 'dp', axis=0, tiled=True)  41.7 us
    psum x1, waiting for transfers between devices, per_device(): lax.psum(key_partial.astype(jnp.bfloat16), 'tensor').astype(jnp.float32)  36.8 us
    all_gather x1, blocking collectives, per_device(): lax.all_gather(output_weight.astype(jnp.bfloat16), 'dp', axis=1, tiled=True)  25 us
  transfers between devices with their start and end apart: 37, of which 11 were waited for; matrix products, arithmetic and copies ran while one was open for 20% of the time, Pallas kernels for 0%

commit v1 on v0

v1 whole, which is shorter than its diff:
```python
import functools

import jax
import jax.numpy as jnp
import numpy as np
from jax import lax
from jax.experimental import pallas as pl
from jax.experimental.pallas import tpu as pltpu
from jax.sharding import PartitionSpec as P

D = 1152
H = 4
HD = 256
FF = 6912
STEP = 10


norm_epsilon = 1e-06
rope_base = 1000000.0
beta_first = 0.9
beta_second = 0.95
adam_epsilon = 1e-08
weight_decay = 0.1
matrix_rate = 2.0
gain_rate = 1.0


def adam_update(weight, gradient, first, second, rate, decay_rate):
    first_new = beta_first * first + (1.0 - beta_first) * gradient
    second_new = beta_second * second + (1.0 - beta_second) * gradient * gradient
    first_hat = first_new / (1.0 - beta_first**STEP)
    second_hat = second_new / (1.0 - beta_second**STEP)
    weight_new = weight - rate * (
        first_hat / (jnp.sqrt(second_hat) + adam_epsilon) + decay_rate * weight
    )
    return (first_new, second_new, weight_new)


FP = 1792
QKVO, FFN, QKVO_REST, FFN_REST, DOWN = range(5)
GATE_UP = FFN
WIDTHS = (1024, 3 * FP, 1152, 3 * FP)
LEAD = (2, 2, 4, 4, 16)
REST_LEAD = (2, 4, 16)
SAVED = (
    (LEAD + (WIDTHS[QKVO],), jnp.bfloat16),
    (REST_LEAD + (WIDTHS[QKVO_REST],), jnp.bfloat16),
    ((4, 128, D), jnp.bfloat16),
    ((512, HD), jnp.float32),
    ((512, HD), jnp.float32),
    ((512, HD), jnp.bfloat16),
    ((512, HD), jnp.bfloat16),
    ((512, HD), jnp.bfloat16),
    ((512, 512), jnp.float32),
    ((4, 128, HD), jnp.bfloat16),
    ((4, 128, D), jnp.bfloat16),
    ((512, HD // 2), jnp.float32),
    ((512, HD // 2), jnp.float32),
)
MESH = pl.DeviceIdType.MESH
LOW = jnp.bfloat16
F32 = jnp.float32
VMEM_LIMIT = 58 * 1024 * 1024


def order_row():
    p = lax.broadcasted_iota(jnp.int32, (1, D), 1)
    rest = p >= 1024
    a = jnp.where(rest, (p >> 4) & 3, (p >> 6) & 3)
    b = jnp.where(rest, (p >> 2) & 3, (p >> 4) & 3)
    c = jnp.where(rest, (p >> 6) & 1, (p >> 8) & 1)
    second = (p >= 512) & (p < 1024)
    z, x = jnp.where(second, b, a), jnp.where(second, a, b)
    row = jnp.where(rest, 32 + (p & 3), (p & 15) + jnp.where(second, 16, 0))
    return ((z * 4 + x) * 2 + c) * 36 + row


def gain_row(n, order):
    p = lax.broadcasted_iota(jnp.int32, (1, D), 1)
    flat = n * D + (order if n < 4 else p)
    dp = jnp.floor((flat.astype(jnp.float32) + 0.5) * (1.0 / 160.0)).astype(jnp.int32)
    entry = flat - dp * 160
    spot = (dp & 1) * 16 + (dp >> 3) * 4 + ((dp >> 1) & 3)
    holder = spot * 4 + jnp.where(entry >= 128, 1, 0)
    if n == 4:
        holder = jnp.where(p < 2 * HD, holder, 128)
    return holder, entry & 127


def place():
    dp = lax.axis_index("dp")
    return dp // 8, (dp // 2) % 4, dp % 2, lax.axis_index("tensor")


def neighbour(h, z, x, c, y, ds, df, other=False):
    dz, dx = (ds, df) if h == 0 else (df, ds)
    core = 1 - c if other else c
    return ((((z + dz) % 4) * 4 + (x + dx) % 4) * 2 + core, y)


def along(y, step):
    return (lax.axis_index("dp"), (y + step) % 4)


def greet(z, x, c, y, planes, rings, far=False):
    devices = []
    if planes:
        for h, df, other in (
            (0, 1, False),
            (0, -1, False),
            (1, 1, False),
            (1, -1, False),
            (0, 0, True),
        ):
            devices.append(neighbour(h, z, x, c, y, 0, df, other))
    if rings:
        devices += [along(y, 1), along(y, 3)]
    if far:
        devices.append(along(y, 2))
    barrier = pltpu.get_barrier_semaphore()
    for device in devices:
        pl.semaphore_signal(barrier, inc=1, device_id=device, device_id_type=MESH)
    return lambda: pl.semaphore_wait(barrier, len(devices))


class Sender:
    def __init__(self, send, recv):
        self.send, self.recv, self.started = send, recv, []

    def push(self, at, source, target, device):
        copy = pltpu.make_async_remote_copy(
            src_ref=source,
            dst_ref=target,
            send_sem=self.send.at[at],
            recv_sem=self.recv.at[at],
            device_id=device,
            device_id_type=MESH,
        )
        copy.start()
        self.started.append(copy)
        return copy

    def close(self):
        for copy in self.started:
            copy.wait_send()


def split(width):
    return (width // 128 + 1) // 2 * 128


def nt(a, b):
    return lax.dot_general(a, b, (((1,), (1,)), ((), ())), preferred_element_type=F32)


def nn(a, b):
    return jnp.dot(a, b, preferred_element_type=F32)


def rms_scale(u):
    return lax.rsqrt(jnp.mean(u * u, axis=-1, keepdims=True) + norm_epsilon)


def rms_back(u, gain, e):
    r = rms_scale(u)
    unit = u * r
    scaled = e * gain
    inner = jnp.mean(scaled * unit, axis=-1, keepdims=True)
    return r * (scaled - unit * inner), jnp.sum(e * unit, axis=0, keepdims=True)


def turn(values, cosine, sine):
    former, latter = values[:, : HD // 2], values[:, HD // 2 :]
    return jnp.concatenate(
        [former * cosine - latter * sine, latter * cosine + former * sine], axis=1
    )


class RingGather:
    def __init__(self, sender, slot, y, full):
        self.sender, self.slot, self.y, self.full = sender, slot, y, full
        self.half = full.shape[1] // 2

    def start(self):
        block = self.full.at[self.y]
        self.from_left = self.sender.push((self.slot, 0), block, block, along(self.y, 1))
        self.from_right = self.sender.push((self.slot, 1), block, block, along(self.y, 3))

    def forward(self):
        self.from_left.wait_recv()
        part = self.full.at[(self.y + 3) % 4, pl.ds(0, self.half)]
        self.far_left = self.sender.push((self.slot, 2), part, part, along(self.y, 1))
        self.from_right.wait_recv()
        part = self.full.at[(self.y + 1) % 4, pl.ds(self.half, self.half)]
        self.far_right = self.sender.push((self.slot, 3), part, part, along(self.y, 3))

    def finish(self):
        self.far_left.wait_recv()
        self.far_right.wait_recv()


class RingReduce:
    def __init__(self, sender, slot, y, sums, part, halves, wholes):
        self.sender, self.slot, self.y, self.sums = sender, slot, y, sums
        self.part, self.halves, self.wholes = part, halves, wholes
        self.half = part.shape[1] // 2

    def send(self, k, source, target, step):
        return self.sender.push((self.slot, k), source, target, along(self.y, step))

    def begin(self):
        far, half = (self.y + 2) % 4, self.half
        self.part[far] = self.sums[far].astype(LOW)
        self.first = self.send(0, self.part.at[far, pl.ds(0, half)], self.halves.at[0], 1)
        self.second = self.send(1, self.part.at[far, pl.ds(half, half)], self.halves.at[1], 3)

    def middle(self):
        right, left, half = (self.y + 1) % 4, (self.y + 3) % 4, self.half
        self.part[right, half:] = self.sums[right, half:].astype(LOW)
        self.part[left, :half] = self.sums[left, :half].astype(LOW)
        self.first.wait_recv()
        value = self.sums[right, :half] + self.halves[0].astype(F32)
        self.part[right, :half] = value.astype(LOW)
        self.third = self.send(2, self.part.at[right], self.wholes.at[0], 1)
        self.second.wait_recv()
        value = self.sums[left, half:] + self.halves[1].astype(F32)
        self.part[left, half:] = value.astype(LOW)
        self.fourth = self.send(3, self.part.at[left], self.wholes.at[1], 3)

    def end(self):
        self.third.wait_recv()
        self.fourth.wait_recv()
        value = self.sums[self.y] + self.wholes[0].astype(F32)
        return value + self.wholes[1].astype(F32)


def ring_scratch(count, rows):
    return [
        pltpu.VMEM((count, 4, rows, D), F32),
        pltpu.VMEM((count, 4, rows, D), LOW),
        pltpu.VMEM((count, 2, rows // 2, D), LOW),
        pltpu.VMEM((count, 2, rows, D), LOW),
    ]


def fill_shuffle(shuffle):
    order = order_row()

    def body(i, carry):
        first = pl.multiple_of(i * 128, 128)
        rows = lax.broadcasted_iota(jnp.int32, (128, D), 0) + first
        shuffle[pl.ds(first, 128)] = jnp.where(rows == order, 1.0, 0.0).astype(LOW)
        return carry

    lax.fori_loop(0, 9, body, 0)


class PlaneGather:
    def __init__(self, sender, local, p, own, full, at):
        self.sender, self.local, self.p, self.own, self.full = sender, local, p, own, full
        self.at = at
        self.copies = {}

    def spot(self, h):
        z, x, c, y = self.at
        return (z, x) if h == 0 else (x, z)

    def send(self, h, k, source, target, ds, df, other=False):
        self.copies[h, k] = self.sender.push(
            (self.p, h, k), source, target, neighbour(h, *self.at, ds, df, other)
        )

    def start(self):
        c = self.at[2]
        for h in range(2):
            s, f = self.spot(h)
            mine = self.full.at[h, c, s, f]
            self.send(h, 0, self.own.at[h], mine, 0, 1)
            self.send(h, 1, self.own.at[h], mine, 0, -1)
            keep = pltpu.make_async_copy(self.own.at[h], mine, self.local.at[self.p, h])
            keep.start()
            self.copies[h, "own"] = keep

    def forward(self):
        c = self.at[2]
        width = self.own.shape[-1]
        cut = split(width)
        for h in range(2):
            s, f = self.spot(h)
            for k, df, lanes in ((0, -1, pl.ds(0, cut)), (1, 1, pl.ds(cut, width - cut))):
                self.copies[h, k].wait_recv()
                block = self.full.at[h, c, s, (f + df) % 4, :, lanes]
                self.send(h, k + 2, block, block, 0, -df)

    def start_slabs(self):
        c = self.at[2]
        for h in range(2):
            s, f = self.spot(h)
            self.copies[h, "own"].wait()
            self.copies[h, 2].wait_recv()
            self.copies[h, 3].wait_recv()
            slab = self.full.at[h, c, s]
            self.send(h, 4, slab, slab, 1, 0)
            self.send(h, 5, slab, slab, -1, 0)
            self.send(h, 8, slab, slab, 0, 0, True)

    def forward_slabs(self):
        c = self.at[2]
        for h in range(2):
            s, f = self.spot(h)
            for k, ds, first in ((4, -1, 0), (5, 1, 2)):
                self.copies[h, k].wait_recv()
                slab = self.full.at[h, c, (s + ds) % 4]
                part = self.full.at[h, c, (s + ds) % 4, pl.ds(first, 2)]
                self.send(h, k + 2, part, part, -ds, 0)
                self.send(h, k + 5, slab, slab, 0, 0, True)

    def last_slabs(self):
        c = self.at[2]
        for h in range(2):
            s, f = self.spot(h)
            self.copies[h, 6].wait_recv()
            self.copies[h, 7].wait_recv()
            slab = self.full.at[h, c, (s + 2) % 4]
            self.send(h, 11, slab, slab, 0, 0, True)

    def finish(self):
        for h in range(2):
            for k in (8, 9, 10, 11):
                self.copies[h, k].wait_recv()


class PlaneReduce:
    def __init__(self, sender, p, source, mine, buffers, out, at):
        self.sender, self.p, self.source, self.mine = sender, p, source, mine
        self.other, self.half_slab, self.whole_slab, self.half_block, self.whole_block = buffers
        self.out, self.at, self.copies = out, at, {}
        self.keep = None

    def spot(self, h):
        z, x, c, y = self.at
        return (z, x) if h == 0 else (x, z)

    def send(self, h, k, source, target, ds, df, other=False):
        self.copies[h, k] = self.sender.push(
            (self.p, h, k), source, target, neighbour(h, *self.at, ds, df, other)
        )

    def swap(self, local=None):
        c = self.at[2]
        if local is not None:
            self.keep = []
            for h in range(2):
                copy = pltpu.make_async_copy(
                    self.source(h, c), self.mine(h), local.at[self.p, h]
                )
                copy.start()
                self.keep.append(copy)
        for k, ds in ((0, 2), (9, 1), (10, -1), (11, 0)):
            for h in range(2):
                to = (self.spot(h)[0] + ds) % 4
                slab = self.source(h, 1 - c).at[to]
                self.send(h, k, slab, self.other.at[h, to], 0, 0, True)

    def slabs_far(self):
        for h in range(2):
            s, f = self.spot(h)
            mine = self.mine(h)
            if self.keep is not None:
                self.keep[h].wait()
            self.copies[h, 0].wait_recv()
            far = (s + 2) % 4

            def both(b, carry, h=h, mine=mine, far=far):
                total = mine[far, b].astype(F32) + self.other[h, far, b].astype(F32)
                mine[far, b] = total.astype(LOW)
                return carry

            lax.fori_loop(0, 4, both, 0)
            self.send(h, 1, mine.at[far, pl.ds(0, 2)], self.half_slab.at[h, 0], 1, 0)
            self.send(h, 2, mine.at[far, pl.ds(2, 2)], self.half_slab.at[h, 1], -1, 0)

    def slabs_near(self):
        for h in range(2):
            s, f = self.spot(h)
            mine = self.mine(h)
            for k, ds, first in ((1, 1, 0), (2, -1, 2)):
                self.copies[h, k + 8].wait_recv()
                self.copies[h, k].wait_recv()
                to = (s + ds) % 4
                for b in range(4):
                    total = mine[to, b].astype(F32) + self.other[h, to, b].astype(F32)
                    if first <= b < first + 2:
                        total = total + self.half_slab[h, k - 1, b - first].astype(F32)
                    mine[to, b] = total.astype(LOW)
                self.send(h, k + 2, mine.at[to], self.whole_slab.at[h, k - 1], ds, 0)

    def blocks_far(self):
        width = self.out.shape[-1]
        cut = split(width)
        for h in range(2):
            s, f = self.spot(h)
            mine = self.mine(h)
            self.copies[h, 11].wait_recv()
            self.copies[h, 3].wait_recv()
            self.copies[h, 4].wait_recv()

            def three(b, carry, h=h, s=s, mine=mine):
                total = mine[s, b].astype(F32) + self.other[h, s, b].astype(F32)
                total = total + self.whole_slab[h, 0, b].astype(F32)
                mine[s, b] = (total + self.whole_slab[h, 1, b].astype(F32)).astype(LOW)
                return carry

            lax.fori_loop(0, 4, three, 0)
            far = (f + 2) % 4
            self.send(
                h,
                5,
                mine.at[s, far, :, pl.ds(0, cut)],
                self.half_block.at[h, 0],
                0,
                1,
            )
            self.send(
                h,
                6,
                mine.at[s, far, :, pl.ds(cut, width - cut)],
                self.half_block.at[h, 1, :, pl.ds(0, width - cut)],
                0,
                -1,
            )

    def blocks_near(self):
        width = self.out.shape[-1]
        cut = split(width)
        for h in range(2):
            s, f = self.spot(h)
            mine = self.mine(h)
            for k, df, first, size in ((5, 1, 0, cut), (6, -1, cut, width - cut)):
                self.copies[h, k].wait_recv()
                to = (f + df) % 4
                lanes = slice(first, first + size)
                mine[s, to, :, lanes] = (
                    mine[s, to, :, lanes].astype(F32)
                    + self.half_block[h, k - 5, :, :size].astype(F32)
                ).astype(LOW)
                self.send(h, k + 2, mine.at[s, to], self.whole_block.at[h, k - 5], 0, df)

    def finish(self):
        for h in range(2):
            s, f = self.spot(h)
            self.copies[h, 7].wait_recv()
            self.copies[h, 8].wait_recv()
            total = self.mine(h)[s, f].astype(F32) + self.whole_block[h, 0].astype(F32)
            self.out[h] = total + self.whole_block[h, 1].astype(F32)


class RestGather(PlaneGather):
    def __init__(self, sender, p, own, near, full, at):
        super().__init__(sender, None, p, own, full, at)
        self.near = near
        self.cut = split(own.shape[-1])
        self.lanes = (pl.ds(0, self.cut), pl.ds(self.cut, own.shape[-1] - self.cut))

    def start(self):
        x = self.at[1]
        self.near[x] = self.own[...]
        self.send(0, 0, self.own, self.near.at[x], 0, 1)
        self.send(0, 1, self.own, self.near.at[x], 0, -1)

    def forward(self):
        x = self.at[1]
        for k, df in ((0, -1), (1, 1)):
            self.copies[0, k].wait_recv()
            block = self.near.at[(x + df) % 4, :, self.lanes[k]]
            self.send(0, k + 2, block, block, 0, -df)

    def start_slabs(self):
        z, x, c, y = self.at
        self.copies[0, 2].wait_recv()
        self.copies[0, 3].wait_recv()
        self.full[c, z] = self.near[...].reshape(16, self.near.shape[-1])
        slab = self.full.at[c, z]
        self.send(0, 4, slab, slab, 1, 0)
        self.send(0, 5, slab, slab, -1, 0)
        self.send(0, 8, slab, slab, 0, 0, True)

    def forward_slabs(self):
        z, x, c, y = self.at
        for k, ds in ((4, -1), (5, 1)):
            self.copies[0, k].wait_recv()
            slab = self.full.at[c, (z + ds) % 4]
            part = self.full.at[c, (z + ds) % 4, :, self.lanes[k - 4]]
            self.send(0, k + 2, part, part, -ds, 0)
            self.send(0, k + 5, slab, slab, 0, 0, True)

    def last_slabs(self):
        z, x, c, y = self.at
        self.copies[0, 6].wait_recv()
        self.copies[0, 7].wait_recv()
        slab = self.full.at[c, (z + 2) % 4]
        self.send(0, 11, slab, slab, 0, 0, True)

    def finish(self):
        for k in (8, 9, 10, 11):
            self.copies[0, k].wait_recv()


class RestReduce:
    def __init__(self, sender, p, source, mine, buffers, out, at):
        self.sender, self.p, self.source, self.mine = sender, p, source, mine
        self.other, self.half_slab, self.whole_slab = buffers[:3]
        self.blocks, self.half_block, self.whole_block = buffers[3:]
        self.out, self.at, self.copies = out, at, {}
        self.keep = None
        width = out.shape[-1]
        cut = split(width)
        self.cuts = ((0, cut), (cut, width - cut))

    def send(self, k, source, target, ds, df, other=False):
        self.copies[k] = self.sender.push(
            (self.p, 0, k), source, target, neighbour(0, *self.at, ds, df, other)
        )

    def swap(self, local=None):
        c = self.at[2]
        self.send(0, self.source.at[1 - c], self.other, 0, 0, True)
        if local is not None:
            self.keep = pltpu.make_async_copy(
                self.source.at[c], self.mine, local.at[self.p, 0]
            )
            self.keep.start()

    def slabs_far(self):
        z = self.at[0]
        if self.keep is not None:
            self.keep.wait()
        self.copies[0].wait_recv()
        for s in range(4):
            self.mine[s] = (self.mine[s].astype(F32) + self.other[s].astype(F32)).astype(LOW)
        far = (z + 2) % 4
        for i, (first, size) in enumerate(self.cuts):
            self.send(
                1 + i,
                self.mine.at[far, :, pl.ds(first, size)],
                self.half_slab.at[i, :, pl.ds(0, size)],
                (1, -1)[i],
                0,
            )

    def slabs_near(self):
        z = self.at[0]
        for i, (first, size) in enumerate(self.cuts):
            self.copies[1 + i].wait_recv()
            ds = (1, -1)[i]
            to = (z + ds) % 4
            lanes = slice(first, first + size)
            self.mine[to, :, lanes] = (
                self.mine[to, :, lanes].astype(F32) + self.half_slab[i, :, :size].astype(F32)
            ).astype(LOW)
            self.send(3 + i, self.mine.at[to], self.whole_slab.at[i], ds, 0)

    def blocks_far(self):
        z, x, c, y = self.at
        self.copies[3].wait_recv()
        self.copies[4].wait_recv()
        total = self.mine[z].astype(F32) + self.whole_slab[0].astype(F32)
        total = (total + self.whole_slab[1].astype(F32)).astype(LOW)
        self.blocks[...] = total.reshape(self.blocks.shape)
        far = (x + 2) % 4
        for i, (first, size) in enumerate(self.cuts):
            self.send(
                5 + i,
                self.blocks.at[far, :, pl.ds(first, size)],
                self.half_block.at[i, :, pl.ds(0, size)],
                0,
                (1, -1)[i],
            )

    def blocks_near(self):
        x = self.at[1]
        for i, (first, size) in enumerate(self.cuts):
            self.copies[5 + i].wait_recv()
            df = (1, -1)[i]
            to = (x + df) % 4
            lanes = slice(first, first + size)
            self.blocks[to, :, lanes] = (
                self.blocks[to, :, lanes].astype(F32) + self.half_block[i, :, :size].astype(F32)
            ).astype(LOW)
            self.send(7 + i, self.blocks.at[to], self.whole_block.at[i], 0, df)

    def finish(self):
        x = self.at[1]
        self.copies[7].wait_recv()
        self.copies[8].wait_recv()
        total = self.blocks[x].astype(F32) + self.whole_block[0].astype(F32)
        self.out[...] = total + self.whole_block[1].astype(F32)


def forward_kernel(
    query, keyvalue, output, gate, up, down_t, own_gains, tokens_in, cotangent, doc_row,
    w12, w12r, gains, attention, middle, ffn_full, upstream, *refs
):
    count = len(SAVED)
    saved, kept = refs[:count], refs[count : 2 * count]
    (
        w0, w0r, normed, query_raw, key_raw, query_rot, key_rot, value_low, probs, heads,
        x_full, cosine, sine,
    ) = kept
    (
        own0, own12, own0r, own12r, shuffle, near0, near12, ids, sums, part, halves, wholes,
        send, recv, local, ring_send, ring_recv, save_sem,
    ) = refs[2 * count :]
    z, x, c, y = at = place()
    entered = greet(z, x, c, y, True, True)
    planes = Sender(send, recv)
    rings = Sender(ring_send, ring_recv)
    qkvo = PlaneGather(planes, local, QKVO, own0, w0, at)
    ffn = PlaneGather(planes, local, FFN, own12, w12, at)
    qkvo_rest = RestGather(planes, QKVO_REST, own0r, near0, w0r, at)
    ffn_rest = RestGather(planes, FFN_REST, own12r, near12, w12r, at)
    columns = gate.shape[1]
    for h in range(2):
        rows = slice(16 * h, 16 * h + 16)
        own0[h, :, 0:256] = query[rows].astype(LOW)
        own0[h, :, 256:768] = keyvalue[rows].astype(LOW)
        own0[h, :, 768:1024] = output[rows].astype(LOW)
    own0r[:, 0:256] = query[32:36].astype(LOW)
    own0r[:, 256:768] = keyvalue[32:36].astype(LOW)
    own0r[:, 768:1024] = output[32:36].astype(LOW)
    own0r[:, 1024:1152] = jnp.zeros((4, 128), LOW)
    own0r[0:1, 1024:1152] = own_gains[:, 0:128].astype(LOW)
    own0r[1:2, 1024:1056] = own_gains[:, 128:160].astype(LOW)
    entered()
    qkvo.start()
    qkvo_rest.start()
    for first, matrix in ((0, gate), (FP, up), (2 * FP, down_t)):
        for h in range(2):
            own12[h, :, first : first + columns] = matrix[16 * h : 16 * h + 16].astype(LOW)
            own12[h, :, first + columns : first + FP] = jnp.zeros((16, FP - columns), LOW)
        own12r[:, first : first + columns] = matrix[32:36].astype(LOW)
        own12r[:, first + columns : first + FP] = jnp.zeros((4, FP - columns), LOW)
    qkvo_rest.forward()
    qkvo.forward()
    qkvo_rest.start_slabs()
    qkvo.start_slabs()
    ffn.start()
    ffn_rest.start()
    fill_shuffle(shuffle)
    x_full[y] = nn(tokens_in[...], shuffle[...]).astype(LOW)
    token_ring = RingGather(rings, 0, y, x_full)
    token_ring.start()
    qkvo_rest.forward_slabs()
    qkvo.forward_slabs()
    ffn_rest.forward()
    ffn.forward()
    ffn_rest.start_slabs()
    ffn.start_slabs()
    ids[...] = jnp.broadcast_to(doc_row[...].astype(F32), (128, 512)).T
    live = ids[pl.ds(pl.multiple_of(y * 128, 128), 128), 0:1] >= 0
    upstream[...] = jnp.where(live, nn(cotangent[...], shuffle[...]), 0.0)
    token_ring.forward()
    key_place = lax.broadcasted_iota(jnp.int32, (512, 512), 1).astype(F32)
    starts = jnp.min(
        jnp.where(ids[:, 0:1] == doc_row[...].astype(F32), key_place, 512.0),
        axis=1,
        keepdims=True,
    )
    position = lax.broadcasted_iota(jnp.int32, (512, 1), 0).astype(F32) - starts
    exponent = lax.broadcasted_iota(jnp.int32, (1, HD // 2), 1).astype(F32) * (2.0 / HD)
    angle = position * jnp.exp(exponent * -np.log(rope_base))
    cosine[...] = jnp.cos(angle)
    sine[...] = jnp.sin(angle)
    qkvo_rest.last_slabs()
    qkvo.last_slabs()
    token_ring.finish()
    qkvo_rest.finish()
    held = w0r[:, :, :, 1024:1152].reshape(128, 128)
    rows = lax.broadcasted_iota(jnp.int32, (128, D), 0)
    order = order_row()
    for n in range(5):
        holder, entry = gain_row(n, order)
        pick = jnp.where(rows == entry, 1.0, 0.0).astype(LOW)
        gains[n : n + 1] = jnp.sum(
            jnp.where(rows == holder, nn(held, pick), 0.0), axis=0, keepdims=True
        )
    gains[5:8] = jnp.zeros((3, D), F32)

    def norm_rows(t, carry):
        u = x_full[t].astype(F32)
        normed[t] = (u * rms_scale(u) * gains[0:1]).astype(LOW)
        return carry

    lax.fori_loop(0, 4, norm_rows, 0)
    qkvo.finish()
    weights = w0[:, :, :, :, :, 0:768].reshape(1024, 768)
    rest = w0r[:, :, :, 0:768].reshape(128, 768)
    whole = normed[...].reshape(512, D)
    raw = nn(whole[:, :1024], weights) + nn(whole[:, 1024:], rest)
    query_raw[...] = raw[:, :HD]
    key_raw[...] = raw[:, HD : 2 * HD]
    value_low[...] = raw[:, 2 * HD :].astype(LOW)
    cos, sin = cosine[...], sine[...]
    u = query_raw[...]
    query_rot[...] = turn(u * rms_scale(u) * gains[4:5, :HD], cos, sin).astype(LOW)
    u = key_raw[...]
    key_rot[...] = turn(u * rms_scale(u) * gains[4:5, HD : 2 * HD], cos, sin).astype(LOW)
    scores = nt(query_rot[...], key_rot[...]) * HD ** (-0.5)
    row_index = lax.broadcasted_iota(jnp.int32, (512, 512), 0)
    key_index = lax.broadcasted_iota(jnp.int32, (512, 512), 1)
    own_ids = ids[:, 0:1]
    same = (own_ids == doc_row[...].astype(F32)) & (own_ids >= 0) & (key_index <= row_index)
    scores = jnp.where(same | (key_index == row_index), scores, -1e30)
    exponents = jnp.exp(scores - jnp.max(scores, axis=-1, keepdims=True))
    probs[...] = exponents / jnp.sum(exponents, axis=-1, keepdims=True)
    heads[...] = nn(probs[...].astype(LOW), value_low[...]).astype(LOW).reshape(4, 128, HD)

    saves = [
        pltpu.make_async_copy(source, target, save_sem.at[i])
        for i, (source, target) in enumerate(zip(kept, saved))
    ]
    for save in saves:
        save.start()
    project_main = w0[:, :, :, :, :, 768:1024].reshape(1024, HD)
    project_rest = w0r[:, :, :, 768:1024].reshape(128, HD)
    reducers = []
    for m in range(2):
        block = heads[:, 64 * m : 64 * m + 64].reshape(256, HD)
        sums[m, :, :, :1024] = nt(block, project_main).reshape(4, 64, 1024)
        sums[m, :, :, 1024:] = nt(block, project_rest).reshape(4, 64, 128)
        reducers.append(
            RingReduce(rings, 1 + m, y, sums.at[m], part.at[m], halves.at[m], wholes.at[m])
        )
        reducers[m].begin()
    ffn_rest.forward_slabs()
    reducers[0].middle()
    reducers[1].middle()
    ffn.forward_slabs()
    ffn_rings = []
    for m in range(2):
        mine = slice(64 * m, 64 * m + 64)
        total = reducers[m].end()
        attention[mine] = total
        u = x_full[y, mine].astype(F32) + total * rms_scale(total) * gains[1:2]
        middle[mine] = u
        ffn_full[m, y] = (u * rms_scale(u) * gains[2:3]).astype(LOW)
        ffn_rings.append(RingGather(rings, 3 + m, y, ffn_full.at[m]))
        ffn_rings[m].start()
    ffn_rest.last_slabs()
    ffn_rings[0].forward()
    ffn_rings[1].forward()
    ffn.last_slabs()
    ffn_rings[0].finish()
    ffn_rings[1].finish()
    ffn_rest.finish()
    ffn.finish()
    for save in saves:
        save.wait()
    planes.close()
    rings.close()


def run_forward(held):
    vmem = pl.BlockSpec(memory_space=pltpu.VMEM)
    hbm = pl.BlockSpec(memory_space=pl.ANY)
    shapes = [
        (LEAD + (WIDTHS[FFN],), LOW, hbm),
        (REST_LEAD + (WIDTHS[FFN_REST],), LOW, vmem),
        ((8, D), F32, vmem),
        ((128, D), F32, vmem),
        ((128, D), F32, vmem),
        ((2, 4, 64, D), LOW, vmem),
        ((128, D), F32, vmem),
    ]
    shapes += [(shape, kind, hbm) for shape, kind in SAVED]
    return pl.pallas_call(
        forward_kernel,
        out_shape=[jax.ShapeDtypeStruct(s, t) for s, t, _ in shapes],
        in_specs=[vmem] * len(held),
        out_specs=[m for _, _, m in shapes],
        scratch_shapes=[pltpu.VMEM(shape, kind) for shape, kind in SAVED]
        + [
            pltpu.VMEM((2, 16, WIDTHS[QKVO]), LOW),
            pltpu.VMEM((2, 16, WIDTHS[FFN]), LOW),
            pltpu.VMEM((4, WIDTHS[QKVO_REST]), LOW),
            pltpu.VMEM((4, WIDTHS[FFN_REST]), LOW),
            pltpu.VMEM((D, D), LOW),
            pltpu.VMEM((4, 4, WIDTHS[QKVO_REST]), LOW),
            pltpu.VMEM((4, 4, WIDTHS[FFN_REST]), LOW),
            pltpu.VMEM((512, 128), F32),
        ]
        + ring_scratch(2, 64)
        + [
            pltpu.SemaphoreType.DMA((4, 2, 12)),
            pltpu.SemaphoreType.DMA((4, 2, 12)),
            pltpu.SemaphoreType.DMA((4, 2)),
            pltpu.SemaphoreType.DMA((5, 4)),
            pltpu.SemaphoreType.DMA((5, 4)),
            pltpu.SemaphoreType.DMA((len(SAVED),)),
        ],
        compiler_params=pltpu.CompilerParams(
            collective_id=0, has_side_effects=True, vmem_limit_bytes=VMEM_LIMIT
        ),
        name="gather_and_attend",
    )(*held)


def feed_kernel(
    ffn_full, middle, upstream, attention, gains, w12, w12r,
    block_out, middle_grad, attention_low, gain_part, g12, rest_flat,
    weights, act, slope, hidden, gate_up_low, out_full, turned, stage, shuffle,
    sums, part, halves, wholes, load_sem, store_sem, ring_send, ring_recv,
):
    z, x, c, y = place()
    loads = []
    for i, (first, size) in enumerate(((0, 2 * FP), (2 * FP, FP))):
        lanes = pl.ds(first, size)
        for k, source, row, rows in ((0, w12, 0, 1024), (1, w12r, 1024, 128)):
            load = pltpu.make_async_copy(
                source.at[:, lanes], weights.at[pl.ds(row, rows), lanes], load_sem.at[i, k]
            )
            load.start()
            loads.append(load)
    greet(z, x, c, y, False, True)()
    rings = Sender(ring_send, ring_recv)
    outward = [
        RingReduce(rings, m, y, sums.at[m], part.at[m], halves.at[m], wholes.at[m])
        for m in range(2)
    ]
    gathers = [RingGather(rings, 2 + m, y, out_full.at[m]) for m in range(2)]
    inward = [
        RingReduce(rings, 4 + m, y, sums.at[m], part.at[2 + m], halves.at[2 + m], wholes.at[2 + m])
        for m in range(2)
    ]
    mine = [slice(0, 64), slice(64, 128)]
    loads[0].wait()
    loads[1].wait()

    def chunk(j, first=0):
        return pl.ds(pl.multiple_of(first + j * 256, 256), 256)

    def feed(m, start, stop):
        def body(j, carry):
            lanes = chunk(j)
            rows = ffn_full[m].reshape(256, D)
            gate = nn(rows, weights[:, lanes])
            up = nn(rows, weights[:, chunk(j, FP)])
            t = jnp.tanh(0.7978845608 * gate * (1.0 + 0.044715 * gate * gate))
            hidden[m, :, lanes] = (0.5 * gate * (1.0 + t) * up).astype(LOW)
            act[m, :, lanes] = gate
            slope[m, :, lanes] = up
            return carry

        lax.fori_loop(start, stop, body, 0)

    def down(m):
        sums[m] = nt(hidden[m], weights[:, 2 * FP :]).reshape(4, 64, D)
        outward[m].begin()

    def after(m):
        total = outward[m].end()
        grad, gain = rms_back(total, gains[3:4], upstream[mine[m]])
        out_full[m, y] = grad.astype(LOW)
        gathers[m].start()
        value = middle[mine[m]] + total * rms_scale(total) * gains[3:4]
        return value.astype(LOW), gain

    def slopes(m, start, stop):
        def body(j, carry):
            lanes = chunk(j)
            gate = act[m, :, lanes]
            up = slope[m, :, lanes]
            square = gate * gate
            rise = jnp.tanh(0.7978845608 * gate * (1.0 + 0.044715 * square))
            half = 0.5 * (1.0 + rise)
            bend = 0.7978845608 * (1.0 + 3.0 * 0.044715 * square)
            act[m, :, lanes] = gate * half
            slope[m, :, lanes] = up * (half + 0.5 * gate * (1.0 - rise * rise) * bend)
            return carry

        lax.fori_loop(start, stop, body, 0)

    def hidden_back(m):
        def body(j, carry):
            lanes = chunk(j)
            grad = nn(out_full[m].reshape(256, D), weights[:, chunk(j, 2 * FP)])
            gate_up_low[m, :, lanes] = (grad * slope[m, :, lanes]).astype(LOW)
            gate_up_low[m, :, chunk(j, FP)] = (grad * act[m, :, lanes]).astype(LOW)
            return carry

        lax.fori_loop(0, 7, body, 0)

    def feed_back(m):
        sums[m] = nt(gate_up_low[m], weights[:, : 2 * FP]).reshape(4, 64, D)
        inward[m].begin()

    def weight_grads(left, right, start, stop, offset):
        def body(j, carry):
            slot = j % 2
            lanes = chunk(j, offset)
            copy = pltpu.make_async_copy(
                stage.at[slot], g12.at[:, lanes], store_sem.at[slot]
            )

            @pl.when((j >= 2) | (offset == 0))
            def _():
                copy.wait()

            value = nn(turned[left], right[:, :, chunk(j)].reshape(512, 256)).astype(LOW)
            stage[slot] = value[:1024]
            rest_flat[:, lanes] = value[1024:]
            copy.start()
            return carry

        lax.fori_loop(start, stop, body, 0)

    def before(m):
        total = inward[m].end()
        grad, gain3 = rms_back(middle[mine[m]], gains[2:3], total)
        grad = upstream[mine[m]] + grad
        middle_grad[mine[m]] = grad
        grad, gain2 = rms_back(attention[mine[m]], gains[1:2], grad)
        attention_low[mine[m]] = grad.astype(LOW)
        return gain2, gain3

    feed(0, 0, 7)
    loads[2].wait()
    loads[3].wait()
    down(0)
    feed(1, 0, 3)
    outward[0].middle()
    feed(1, 3, 7)
    down(1)
    out0, gain40 = after(0)
    slopes(0, 0, 7)
    outward[1].middle()
    slopes(1, 0, 4)
    gathers[0].forward()
    slopes(1, 4, 7)
    out1, gain41 = after(1)
    gain_part[3:4] = gain40 + gain41
    gathers[0].finish()
    hidden_back(0)
    gathers[1].forward()
    feed_back(0)
    turned[0] = ffn_full[...].reshape(512, D).T
    gathers[1].finish()
    hidden_back(1)
    inward[0].middle()
    feed_back(1)
    turned[1] = out_full[...].reshape(512, D).T
    weight_grads(1, hidden, 0, 7, 2 * FP)
    inward[1].middle()
    weight_grads(0, gate_up_low, 0, 7, 0)
    fill_shuffle(shuffle)
    block_out[...] = nt(jnp.concatenate([out0, out1], axis=0), shuffle[...]).astype(LOW)
    gain20, gain30 = before(0)
    weight_grads(0, gate_up_low, 7, 14, 0)
    gain21, gain31 = before(1)
    gain_part[1:2] = gain20 + gain21
    gain_part[2:3] = gain30 + gain31
    gain_part[0:1] = jnp.zeros((1, D), F32)
    gain_part[4:8] = jnp.zeros((4, D), F32)
    for slot in range(2):
        pltpu.make_async_copy(
            stage.at[slot], g12.at[:, pl.ds(0, 256)], store_sem.at[slot]
        ).wait()
    rings.close()


def run_feed(ffn_full, middle, upstream, attention, gains, w12, w12r):
    vmem = pl.BlockSpec(memory_space=pltpu.VMEM)
    hbm = pl.BlockSpec(memory_space=pl.ANY)
    shapes = [
        ((128, D), LOW, vmem),
        ((128, D), F32, vmem),
        ((128, D), LOW, vmem),
        ((8, D), F32, vmem),
        ((1024, 3 * FP), LOW, hbm),
        ((128, 3 * FP), LOW, vmem),
    ]
    return pl.pallas_call(
        feed_kernel,
        out_shape=[jax.ShapeDtypeStruct(s, t) for s, t, _ in shapes],
        in_specs=[vmem] * 5 + [hbm] * 2,
        out_specs=[m for _, _, m in shapes],
        scratch_shapes=[
            pltpu.VMEM((D, 3 * FP), LOW),
            pltpu.VMEM((2, 256, FP), F32),
            pltpu.VMEM((2, 256, FP), F32),
            pltpu.VMEM((2, 256, FP), LOW),
            pltpu.VMEM((2, 256, 2 * FP), LOW),
            pltpu.VMEM((2, 4, 64, D), LOW),
            pltpu.VMEM((2, D, 512), LOW),
            pltpu.VMEM((2, 1024, 256), LOW),
            pltpu.VMEM((D, D), LOW),
            pltpu.VMEM((2, 4, 64, D), F32),
            pltpu.VMEM((4, 4, 64, D), LOW),
            pltpu.VMEM((4, 2, 32, D), LOW),
            pltpu.VMEM((4, 2, 64, D), LOW),
            pltpu.SemaphoreType.DMA((2, 2)),
            pltpu.SemaphoreType.DMA((2,)),
            pltpu.SemaphoreType.DMA((6, 4)),
            pltpu.SemaphoreType.DMA((6, 4)),
        ],
        compiler_params=pltpu.CompilerParams(
            collective_id=1, has_side_effects=True, vmem_limit_bytes=VMEM_LIMIT
        ),
        name="feed_forward_and_back",
    )(
        ffn_full,
        middle,
        upstream,
        attention,
        gains,
        w12.reshape(1024, 3 * FP),
        w12r.reshape(128, 3 * FP),
    )


def backward_kernel(*refs):
    attention_low, middle_grad, gains, gain_part, g12, g12r = refs[:6]
    count = len(SAVED)
    saved = refs[6 : 6 + count]
    refs = refs[6 + count :]
    token_grad, out0, out0r, out_g, out12r, out_d, kv_sum, rest_sum = refs[:8]
    kept, refs = refs[8 : 8 + count], refs[8 + count :]
    (
        w0, w0r, normed, query_raw, key_raw, query_rot, key_rot, value_low, probs, heads,
        x_full, cosine, sine,
    ) = kept
    part0, part0r, mine_g, mine12r, mine_d = refs[:5]
    buffers = [refs[5:10], refs[10:15], refs[15:21], refs[21:27], refs[27:32]]
    (
        shuffle, a_full, qkv_low, turned, sums, part, halves, wholes, kv_all, rest_all,
        send, recv, local, ring_send, ring_recv, last_send, last_recv, load_sem,
    ) = refs[32:]
    z, x, c, y = at = place()
    loads = [
        pltpu.make_async_copy(source, target, load_sem.at[i])
        for i, (source, target) in enumerate(zip(saved, kept))
    ]
    for load in loads:
        load.start()
    greet(z, x, c, y, True, True, True)()
    planes = Sender(send, recv)
    rings = Sender(ring_send, ring_recv)
    lasts = Sender(last_send, last_recv)
    qkvo = PlaneReduce(
        planes,
        QKVO,
        lambda h, core: part0.at[h, core],
        lambda h: part0.at[h, c],
        buffers[QKVO],
        out0,
        at,
    )
    gate_up = PlaneReduce(
        planes,
        GATE_UP,
        lambda h, core: g12.at[h, core, :, :, :, pl.ds(0, 2 * FP)],
        lambda h: mine_g.at[h],
        buffers[GATE_UP],
        out_g,
        at,
    )
    down = PlaneReduce(
        planes,
        DOWN,
        lambda h, core: g12.at[h, core, :, :, :, pl.ds(2 * FP, FP)],
        lambda h: mine_d.at[h],
        buffers[DOWN],
        out_d,
        at,
    )
    qkvo_rest = RestReduce(
        planes, QKVO_REST, part0r, part0r.at[c], buffers[QKVO_REST], out0r, at
    )
    ffn_rest = RestReduce(planes, FFN_REST, g12r, mine12r, buffers[FFN_REST], out12r, at)
    a_full[y] = attention_low[...]
    ring = RingGather(rings, 0, y, a_full)
    ring.start()
    down.swap(local)
    ffn_rest.swap(local)
    gate_up.swap(local)
    fill_shuffle(shuffle)
    loads[2].wait()
    turned[0] = normed[...].reshape(512, D).T
    down.slabs_far()
    ring.forward()
    gate_up.slabs_far()
    for i, load in enumerate(loads):
        if i != 2:
            load.wait()
    ring.finish()
    whole = a_full[...].reshape(512, D)
    heads_low = nn(whole[:, :1024], w0[:, :, :, :, :, 768:1024].reshape(1024, HD))
    heads_low = heads_low + nn(
        whole[:, 1024:], w0r[:, :, :, 768:1024].reshape(128, HD)
    )
    heads_low = heads_low.astype(LOW)
    down.slabs_near()
    ffn_rest.slabs_far()
    p = probs[...]
    probs_grad = nt(heads_low, value_low[...])
    score = p * (probs_grad - jnp.sum(p * probs_grad, axis=-1, keepdims=True))
    score_low = score.astype(LOW)
    scale = HD ** (-0.5)
    cos, sin = cosine[...], -sine[...]
    query_grad = turn(nn(score_low, key_rot[...]) * scale, cos, sin)
    key_grad = turn(nn(score_low.T, query_rot[...]) * scale, cos, sin)
    value_grad = nn(p.astype(LOW).T, heads_low)
    gate_up.slabs_near()
    query_grad, query_gain = rms_back(query_raw[...], gains[4:5, :HD], query_grad)
    key_grad, key_gain = rms_back(key_raw[...], gains[4:5, HD : 2 * HD], key_grad)
    qkv_low[:, :, :HD] = query_grad.astype(LOW).reshape(4, 128, HD)
    qkv_low[:, :, HD : 2 * HD] = key_grad.astype(LOW).reshape(4, 128, HD)
    qkv_low[:, :, 2 * HD :] = value_grad.astype(LOW).reshape(4, 128, HD)
    down.blocks_far()
    ffn_rest.slabs_near()
    block = qkv_low[...].reshape(512, 768)
    main = nt(block, w0[:, :, :, :, :, 0:768].reshape(1024, 768))
    sums[:, :, :1024] = main.reshape(4, 128, 1024)
    rest = nt(block, w0r[:, :, :, 0:768].reshape(128, 768))
    sums[:, :, 1024:] = rest.reshape(4, 128, 128)
    reducer = RingReduce(rings, 1, y, sums, part, halves, wholes)
    reducer.begin()
    down.blocks_near()
    turned[1] = a_full[...].reshape(512, D).T
    for j in range(4):
        lanes = slice(j * 256, j * 256 + 256)
        if j < 3:
            value = nn(turned[0], qkv_low[:, :, lanes].reshape(512, 256))
        else:
            value = nn(turned[1], heads[...].reshape(512, 256))
        value = value.astype(LOW)
        part0[:, :, :, :, :, lanes] = value[:1024].reshape(LEAD + (256,))
        part0r[:, :, :, lanes] = value[1024:].reshape(REST_LEAD + (256,))
    qkvo.swap()
    reducer.middle()

    def first_gain(t, carry):
        u = x_full[t].astype(F32)
        return carry + jnp.sum(sums[t] * (u * rms_scale(u)), axis=0, keepdims=True)

    gain = lax.fori_loop(0, 4, first_gain, jnp.zeros((1, D), F32))
    rows = lax.broadcasted_iota(jnp.int32, (128, D), 0)
    order = order_row()
    shares = jnp.zeros((128, 128), F32)
    wide = [gain, gain_part[1:2], gain_part[2:3], gain_part[3:4]]
    wide.append(jnp.concatenate([query_gain, key_gain, jnp.zeros((1, D - 2 * HD), F32)], axis=1))
    for n in range(5):
        holder, entry = gain_row(n, order)
        pick = jnp.where(rows == entry, 1.0, 0.0).astype(LOW)
        placed = jnp.where(rows == holder, wide[n], 0.0).astype(LOW)
        shares = shares + nt(placed, pick)
    part0r[:, :, :, 1024:1152] = shares.astype(LOW).reshape(REST_LEAD + (128,))
    qkvo_rest.swap()
    qkvo.slabs_far()
    ffn_rest.blocks_far()
    qkvo_rest.slabs_far()
    gate_up.blocks_far()
    qkvo.slabs_near()
    qkvo_rest.slabs_near()
    total = reducer.end()
    u = x_full[y].astype(F32)
    grad, gain = rms_back(u, gains[0:1], total)
    grad = (middle_grad[...] + grad).astype(LOW)
    ffn_rest.blocks_near()
    gate_up.blocks_near()
    qkvo.blocks_far()
    qkvo_rest.blocks_far()
    token_grad[...] = nt(grad, shuffle[...]).astype(LOW)
    down.finish()
    qkvo.blocks_near()
    qkvo_rest.blocks_near()
    ffn_rest.finish()
    gate_up.finish()
    qkvo.finish()
    kv_all[y] = out0[:, :, HD : 3 * HD]
    last = []
    for step in (1, 2, 3):
        block = kv_all.at[y]
        last.append(lasts.push((0, step - 1), block, block, along(y, step)))
    qkvo_rest.finish()
    rest_all[y] = out0r[...]
    for step in (1, 2, 3):
        block = rest_all.at[y]
        last.append(lasts.push((1, step - 1), block, block, along(y, step)))
    for copy in last:
        copy.wait_recv()
    kv_sum[...] = kv_all[0] + kv_all[1] + kv_all[2] + kv_all[3]
    rest_sum[...] = rest_all[0] + rest_all[1] + rest_all[2] + rest_all[3]
    planes.close()
    rings.close()
    lasts.close()


def run_backward(held, weight_parts):
    vmem = pl.BlockSpec(memory_space=pltpu.VMEM)
    hbm = pl.BlockSpec(memory_space=pl.ANY)
    shapes = [
        ((128, D), LOW),
        ((2, 16, WIDTHS[QKVO]), F32),
        ((4, WIDTHS[QKVO_REST]), F32),
        ((2, 16, 2 * FP), F32),
        ((4, WIDTHS[FFN_REST]), F32),
        ((2, 16, FP), F32),
        ((2, 16, 2 * HD), F32),
        ((4, WIDTHS[QKVO_REST]), F32),
    ]
    def plane_scratch(width):
        return [
            pltpu.VMEM((2, 4, 4, 16, width), LOW),
            pltpu.VMEM((2, 2, 2, 16, width), LOW),
            pltpu.VMEM((2, 2, 4, 16, width), LOW),
            pltpu.VMEM((2, 2, 16, split(width)), LOW),
            pltpu.VMEM((2, 2, 16, width), LOW),
        ]

    scratch = [pltpu.VMEM(shape, kind) for shape, kind in SAVED]
    scratch += [
        pltpu.VMEM(LEAD + (WIDTHS[QKVO],), LOW),
        pltpu.VMEM(REST_LEAD + (WIDTHS[QKVO_REST],), LOW),
        pltpu.VMEM((2, 4, 4, 16, 2 * FP), LOW),
        pltpu.VMEM((4, 16, WIDTHS[FFN_REST]), LOW),
        pltpu.VMEM((2, 4, 4, 16, FP), LOW),
    ]
    scratch += plane_scratch(WIDTHS[QKVO]) + plane_scratch(2 * FP)
    for p in (QKVO_REST, FFN_REST):
        scratch += [
            pltpu.VMEM((4, 16, WIDTHS[p]), LOW),
            pltpu.VMEM((2, 16, split(WIDTHS[p])), LOW),
            pltpu.VMEM((2, 16, WIDTHS[p]), LOW),
            pltpu.VMEM((4, 4, WIDTHS[p]), LOW),
            pltpu.VMEM((2, 4, split(WIDTHS[p])), LOW),
            pltpu.VMEM((2, 4, WIDTHS[p]), LOW),
        ]
    scratch += plane_scratch(FP)
    scratch += [
        pltpu.VMEM((D, D), LOW),
        pltpu.VMEM((4, 128, D), LOW),
        pltpu.VMEM((4, 128, 3 * HD), LOW),
        pltpu.VMEM((2, D, 512), LOW),
        pltpu.VMEM((4, 128, D), F32),
        pltpu.VMEM((4, 128, D), LOW),
        pltpu.VMEM((2, 64, D), LOW),
        pltpu.VMEM((2, 128, D), LOW),
        pltpu.VMEM((4, 2, 16, 2 * HD), F32),
        pltpu.VMEM((4, 4, WIDTHS[QKVO_REST]), F32),
        pltpu.SemaphoreType.DMA((5, 2, 12)),
        pltpu.SemaphoreType.DMA((5, 2, 12)),
        pltpu.SemaphoreType.DMA((5, 2)),
        pltpu.SemaphoreType.DMA((2, 4)),
        pltpu.SemaphoreType.DMA((2, 4)),
        pltpu.SemaphoreType.DMA((2, 3)),
        pltpu.SemaphoreType.DMA((2, 3)),
        pltpu.SemaphoreType.DMA((len(SAVED),)),
    ]
    return pl.pallas_call(
        backward_kernel,
        out_shape=[jax.ShapeDtypeStruct(s, t) for s, t in shapes],
        in_specs=[vmem] * len(held) + [hbm] * len(weight_parts),
        out_specs=[vmem] * len(shapes),
        scratch_shapes=scratch,
        compiler_params=pltpu.CompilerParams(
            collective_id=2, has_side_effects=True, vmem_limit_bytes=VMEM_LIMIT
        ),
        name="attend_back_and_reduce",
    )(*held, *weight_parts)


def adam_kernel(*refs):
    out0, out0r, out_g, out12r, out_d, kv_sum, rest_sum, block_in, token_in = refs[:9]
    state, results = refs[9:30], refs[30:]
    results[0][...] = block_in[...]
    results[1][...] = token_in[...]
    columns = state[9].shape[1]
    places = (
        (out0, out0r, 0, 0, HD, D),
        (kv_sum, rest_sum, 0, HD, 2 * HD, D),
        (out0, out0r, 3 * HD, 3 * HD, HD, H * HD),
        (out_g, out12r, 0, 0, columns, D),
        (out_g, out12r, FP, FP, columns, D),
        (out_d, out12r, 0, 2 * FP, columns, FF),
    )
    for i, (main, rest, first, rest_first, width, fan_in) in enumerate(places):
        weight, moment, second = state[3 * i : 3 * i + 3]
        for h in range(3):
            rows = slice(16 * h, min(16 * h + 16, 36))
            if h < 2:
                gradient = main[h, :, first : first + width]
            else:
                gradient = rest[:, rest_first : rest_first + width]
            updated = adam_update(
                weight[rows],
                gradient,
                moment[rows],
                second[rows],
                matrix_rate * fan_in ** (-0.5),
                weight_decay,
            )
            for k in range(3):
                results[2 + 3 * i + k][rows] = updated[k]
    gradient = jnp.concatenate([rest_sum[0:1, 1024:1152], rest_sum[1:2, 1024:1056]], axis=1)
    updated = adam_update(
        state[18][...], gradient, state[19][...], state[20][...], gain_rate, 0.0
    )
    for k in range(3):
        results[20 + k][...] = updated[k]


def run_adam(gradients, tokens, state):
    shapes = [(v.shape, v.dtype) for v in tokens]
    for i in range(0, len(state), 3):
        shapes += [(state[i].shape, F32)] * 3
    return pl.pallas_call(
        adam_kernel,
        out_shape=[jax.ShapeDtypeStruct(shape, kind) for shape, kind in shapes],
        compiler_params=pltpu.CompilerParams(vmem_limit_bytes=VMEM_LIMIT),
        name="adam",
    )(*gradients, *tokens, *state)


def per_device(
    tokens,
    document_ids,
    cotangent,
    query_weight,
    keyvalue_weight,
    output_weight,
    gate_weight,
    up_weight,
    down_weight,
    norm_gains,
    query_first,
    query_second,
    keyvalue_first,
    keyvalue_second,
    output_first,
    output_second,
    gate_first,
    gate_second,
    up_first,
    up_second,
    down_first,
    down_second,
    gain_first,
    gain_second,
):
    w12, w12r, gains, attention, middle, ffn_full, upstream, *saved = run_forward(
        (
            query_weight, keyvalue_weight, output_weight.T, gate_weight, up_weight,
            down_weight.T, norm_gains[None, :], tokens, cotangent, document_ids[None, :],
        )
    )
    block_output, middle_grad, attention_low, gain_part, g12, g12r = run_feed(
        ffn_full, middle, upstream, attention, gains, w12, w12r
    )
    token_grad, *gradients = run_backward(
        (attention_low, middle_grad, gains, gain_part),
        (
            g12.reshape(LEAD + (WIDTHS[FFN],)),
            g12r.reshape(REST_LEAD + (WIDTHS[FFN_REST],)),
            *saved,
        ),
    )
    (
        block_output, token_grad, query_next, query_one, query_two, keyvalue_next, keyvalue_one,
        keyvalue_two, output_next, output_one, output_two, gate_next, gate_one, gate_two,
        up_next, up_one, up_two, down_next, down_one, down_two, gain_next, gain_one, gain_two,
    ) = run_adam(
        gradients,
        (block_output, token_grad),
        (
            query_weight, query_first, query_second,
            keyvalue_weight, keyvalue_first, keyvalue_second,
            output_weight.T, output_first.T, output_second.T,
            gate_weight, gate_first, gate_second,
            up_weight, up_first, up_second,
            down_weight.T, down_first.T, down_second.T,
            norm_gains[None, :], gain_first[None, :], gain_second[None, :],
        ),
    )
    return (
        block_output, token_grad, query_next, query_one, query_two, keyvalue_next, keyvalue_one,
        keyvalue_two, output_next.T, output_one.T, output_two.T, gate_next, gate_one, gate_two,
        up_next, up_one, up_two, down_next.T, down_one.T, down_two.T,
        gain_next[0], gain_one[0], gain_two[0],
    )


def solution(mesh):
    placed = (
        P(("dp", "tensor"), None),
        P("dp"),
        P(("dp", "tensor"), None),
        P("dp", "tensor"),
        P("dp", None),
        P("tensor", "dp"),
        P("dp", "tensor"),
        P("dp", "tensor"),
        P("tensor", "dp"),
        P("dp"),
        P("dp", "tensor"),
        P("dp", "tensor"),
        P("dp", None),
        P("dp", None),
        P("tensor", "dp"),
        P("tensor", "dp"),
        P("dp", "tensor"),
        P("dp", "tensor"),
        P("dp", "tensor"),
        P("dp", "tensor"),
        P("tensor", "dp"),
        P("tensor", "dp"),
        P("dp"),
        P("dp"),
    )
    return jax.shard_map(
        per_device,
        mesh=mesh,
        in_specs=placed,
        out_specs=(
            P(("dp", "tensor"), None),
            P(("dp", "tensor"), None),
            P("dp", "tensor"),
            P("dp", "tensor"),
            P("dp", "tensor"),
            P("dp", None),
            P("dp", None),
            P("dp", None),
            P("tensor", "dp"),
            P("tensor", "dp"),
            P("tensor", "dp"),
            P("dp", "tensor"),
            P("dp", "tensor"),
            P("dp", "tensor"),
            P("dp", "tensor"),
            P("dp", "tensor"),
            P("dp", "tensor"),
            P("tensor", "dp"),
            P("tensor", "dp"),
            P("tensor", "dp"),
            P("dp"),
            P("dp"),
            P("dp"),
        ),
        check_vma=False,
    )
```

time: 972 us -> 200 us (0.21)
  blocking collectives: 407 us -> 0 us
  waiting for transfers between devices: 293 us -> 0 us
  Pallas kernels: 0 us -> 199 us
  starting transfers between devices: 74.4 us -> 0 us
  matrix products: 66.9 us -> 0 us
  other arithmetic: 53.1 us -> 0 us
  local copies, waits for them, and re-layouts: 50.3 us -> 0 us
  between operations: 17.8 us -> 0.86 us
    unnamed x3 -> x0, blocking collectives: 351 us -> none
    pallas_call x0 -> x4, Pallas kernels: none -> 199 us  [the longest x1 65.7 us: run_forward(): pl.pallas_call(forward_kernel, out_shape=[jax.ShapeDtypeStruct(s, t) for...]
    all_gather x8 -> x0, waiting for transfers between devices: 190 us -> none  [the longest x1 44.2 us: per_device(): lax.all_gather(gate_weight.astype(jnp.bfloat16), 'dp', axis=0, tiled=True)]
    unnamed x24 -> x0, starting transfers between devices: 72.7 us -> none
    dot_general x24 -> x0, matrix products: 66.9 us -> none  [the longest x1 9.7 us: per_device(): jnp.einsum('rd,fd->rf', ffn_out_full, down_full, preferred_element_type=j...]
    reduce_scatter x4 -> x0, waiting for transfers between devices: 66.1 us -> none  [the longest x1 24 us: per_device(): lax.psum_scatter(jnp.dot(hidden_low, down_full, preferred_element_type=jn...]
    unnamed x208 -> x0, local copies, waits for them, and re-layouts: 49.9 us -> none
    all_gather x2 -> x0, blocking collectives: 46.8 us -> none  [the longest x1 25 us: per_device(): lax.all_gather(output_weight.astype(jnp.bfloat16), 'dp', axis=1, tiled=True)]
  transfers between devices with their start and end apart: 37 -> 0, of which waited for: 11 -> 0; matrix products, arithmetic and copies ran while one was open for 20% -> 0% of each run, Pallas kernels for 0% -> 0%
where the time goes in v1:
time: 200 us; the launch traced here: 199 us
  Pallas kernels  199 us (100%)
    pallas_call x1, Pallas kernels, run_forward(): pl.pallas_call(forward_kernel, out_shape=[jax.ShapeDtypeStruct(s, t) for...  65.7 us
    pallas_call x1, Pallas kernels, run_backward(): pl.pallas_call(backward_kernel, out_shape=[jax.ShapeDtypeStruct(s, t) for...  64.7 us
    pallas_call x1, Pallas kernels, run_feed(): pl.pallas_call(feed_kernel, out_shape=[jax.ShapeDtypeStruct(s, t) for s,...  63.7 us
    pallas_call x1, Pallas kernels, run_adam(): pl.pallas_call(adam_kernel, out_shape=[jax.ShapeDtypeStruct(shape, kind)...  4.54 us

profile of v1, /device:TPU:0, one launch (start us, length us, event | category | flops | bytes accessed | tf_op | source)
XLA Modules:
  0.0 199.4 jit_solution(8815030600200907447)
XLA Ops:
  0.7 65.7 %gather_and_attend.1 = (bf16[2,2,4,4,16,5376]{5,4,3,2,1,0:T(8,128)(2,1)}, bf16[2,4,16,5376]{3,2,1,0:T(8,128)(2,1)}, f32[8,1152]{1,0:T(8,128)}, f32[128,1152]{1,0...) custom-call(f32[36,256]{1,0:T(8,128)} %refs_9_.1, ...), custom_call_target="tpu_custom_call" | custom-call | tf_op jit(solution)/shard_map/gather_and_attend/pallas_call | solution.py:776
  66.4 63.7 %feed_forward_and_back.1 = (bf16[128,1152]{1,0:T(8,128)(2,1)}, f32[128,1152]{1,0:T(8,128)}, bf16[128,1152]{1,0:T(8,128)(2,1)}, f32[8,1152]{1,0:T(8,128)}, bf16[1...) custom-call(bf16[2,4,64,1152]{3,2,1,0:T(8,128)(2,1)} %get-tuple-element.80.ffn_full, ...), custom_call_target="tpu_custom_call" | custom-call | tf_op jit(solution)/shard_map/feed_forward_and_back/pallas_call | solution.py:982
  130.0 64.7 %attend_back_and_reduce.1 = (bf16[128,1152]{1,0:T(8,128)(2,1)}, f32[2,16,1024]{2,1,0:T(8,128)}, f32[4,1152]{1,0:T(4,128)}, f32[2,16,3584]{2,1,0:T(8,128)}, f32[4...) custom-call(bf16[128,1152]{1,0:T(8,128)(2,1)} %get-tuple-element.87.refs_0_, ...), custom_call_target="tpu_custom_call" | custom-call | tf_op jit(solution)/shard_map/attend_back_and_reduce/pallas_call | solution.py:1260
  194.7 4.5 %adam.1 = (bf16[128,1152]{1,0:T(8,128)(2,1)}, bf16[128,1152]{1,0:T(8,128)(2,1)}, f32[36,256]{1,0:T(8,128)}, f32[36,256]{1,0:T(8,128)}, f32[36,256]{1,0:T(8,128)}...) custom-call(f32[2,16,1024]{2,1,0:T(8,128)} %get-tuple-element.105.re, ...), custom_call_target="tpu_custom_call" | custom-call | tf_op jit(solution)/shard_map/adam/pallas_call | solution.py:1317
